TPU v7x, 256 devices: a whole 4x4x8 slice. The times are simulated.
256 devices in a mesh: node: 32 (over y, x, core), dev: 8 (over z).
Axes of the slice: x: 4, y: 4, z: 8, core: 2. Of those that a mesh axis runs over, the one named last changes fastest.
Arguments:
- element_load: float32 [8, 8, 8, 8, 64, 128], P(None, None, None, 'dev', 'node'), may hold values from -4 to 5
- diffusivity: float32 [8, 64, 128], P('dev', 'node'), may hold values from 0.2 to 5
Outputs:
- solution: float32 [8, 8, 8, 8, 64, 128], P(None, None, None, 'dev', 'node')
All inputs are finite; a program needn't handle non-finite values.
Results may differ from a plain program's by a relative error of at most 0.0003.
Values sent between devices are 32-bit elements; how exact they have to be, the bound alone decides.
A program may use at most 128 MiB of HBM per device.

v0:
```python
import jax
import jax.numpy as jnp
import numpy as np
from jax import lax
from jax.experimental import pallas as pl
from jax.experimental.pallas import tpu as pltpu
from jax.sharding import PartitionSpec as P

PF = 8
PM = 4
PC = 2
SMOOTH_FINE = 3
SMOOTH_MID = 3
COARSE_ITERS = 5
SHIFT_MASS = 0.05
LANES = 128
SUB = 8
MESH = pl.DeviceIdType.MESH

def legendre_values(points, poly_order):
    columns = [points * 0.0 + 1.0, points]
    for degree in range(2, poly_order + 1):
        columns.append(
            ((2 * degree - 1) * points * columns[degree - 1] - (degree - 1) * columns[degree - 2])
            / degree
        )
    return np.stack(columns[: poly_order + 1], axis=1)


def largest_eigen(matrix):
    size_n = matrix.shape[0]
    vector = np.cos(2.7 * np.arange(size_n) + 0.3)
    for power_step in range(4000):
        vector = matrix @ vector
        vector = vector / np.sqrt(np.sum(vector * vector))
    return float(vector @ (matrix @ vector))


def gll_level(poly_order):
    point_count = poly_order + 1
    gll_nodes = np.cos(np.pi * np.arange(point_count) / poly_order)
    for newton_step in range(60):
        values = legendre_values(gll_nodes, poly_order)
        gll_nodes = gll_nodes - (gll_nodes * values[:, poly_order] - values[:, poly_order - 1]) / (
            point_count * values[:, poly_order]
        )
    gll_nodes = np.sort(gll_nodes)
    values = legendre_values(gll_nodes, poly_order)
    top_value = values[:, poly_order]
    weights = 2.0 / (poly_order * point_count * top_value**2)
    deriv_matrix = np.zeros((point_count, point_count))
    for row_index in range(point_count):
        for col_index in range(point_count):
            if row_index != col_index:
                deriv_matrix[row_index, col_index] = top_value[row_index] / (
                    top_value[col_index] * (gll_nodes[row_index] - gll_nodes[col_index])
                )
    deriv_matrix[0, 0] = -poly_order * point_count / 4.0
    deriv_matrix[poly_order, poly_order] = poly_order * point_count / 4.0
    stiffness = deriv_matrix.T @ (weights[:, None] * deriv_matrix)
    diag_ids = np.arange(point_count)
    stiff_diag = stiffness[diag_ids, diag_ids]
    diag_scale = 1.0 / np.sqrt(stiff_diag)
    eig_bound = largest_eigen(diag_scale[:, None] * stiffness * diag_scale[None, :])
    return (gll_nodes, weights, deriv_matrix, stiff_diag, eig_bound)


def interp_table(fine_nodes, coarse_nodes):
    interp_mat = np.ones((fine_nodes.shape[0], coarse_nodes.shape[0]))
    for col_index in range(coarse_nodes.shape[0]):
        for other_index in range(coarse_nodes.shape[0]):
            if other_index != col_index:
                interp_mat[:, col_index] *= (fine_nodes - coarse_nodes[other_index]) / (
                    coarse_nodes[col_index] - coarse_nodes[other_index]
                )
    return interp_mat


class Level:
    def __init__(self, points):
        nodes, w, deriv, stiff_diag, bound = gll_level(points - 1)
        self.points = points
        self.planes = 2 * points - 1
        self.rows = SUB * self.planes
        self.x_rows = SUB * (self.planes if points == SUB else -(-self.planes // 2))
        self.z_rows = SUB * (points if points == SUB else -(-points // 2))
        self.nodes = nodes
        self.w = w
        self.khat = (deriv.T @ (w[:, None] * deriv)) / w[:, None]
        self.kdiag = stiff_diag / w
        self.theta = 0.6 * bound
        self.delta = 0.5 * bound

    def steps(self, count):
        sig = self.theta / self.delta
        rho = 1.0 / sig
        out = []
        for _ in range(count - 1):
            rho_next = 1.0 / (2.0 * sig - rho)
            out.append((float(rho_next * rho), float(2.0 * rho_next / self.delta)))
            rho = rho_next
        return out


def roll_coefs(matrix):
    full = np.zeros((SUB, SUB))
    full[: matrix.shape[0], : matrix.shape[1]] = matrix
    i = np.arange(SUB)
    return [full[i, (i - s) % SUB] for s in range(SUB)]


def two_elements(matrix):
    n, m = matrix.shape
    out = np.zeros((2 * n - 1, 2 * m - 1))
    out[:n, :m] = matrix
    out[n - 1 :, m - 1 :] = matrix
    return out


def plane_sum(points):
    values = np.zeros((2 * points - 1,))
    values[:points] += 1
    values[points - 1 :] += 1
    return values


class Consts:
    def __init__(self):
        self.blocks = []
        self.at = {}
        self.row = 0

    def add(self, name, block):
        block = np.asarray(block, np.float64)
        if block.ndim == 1:
            block = np.broadcast_to(block[:, None], (block.shape[0], LANES))
        assert block.shape[0] % SUB == 0
        self.at[name] = (self.row, block.shape[0])
        self.blocks.append(block)
        self.row += block.shape[0]

    def array(self):
        return np.concatenate(self.blocks, 0).astype(np.float32)


FINE, MID, LOW = Level(PF), Level(PM), Level(PC)
J73 = interp_table(FINE.nodes, MID.nodes)
J31 = interp_table(MID.nodes, LOW.nodes)
R73 = (FINE.w[:, None] * J73 / MID.w[None, :]).T
R31 = (MID.w[:, None] * J31).T
R73Z = two_elements(FINE.w[:, None] * J73 / MID.w[None, :])
R73Z[PF - 1] = 0.0
R73Z[PF - 1, PM - 1] = FINE.w[0] / MID.w[0]
R31Z = two_elements(MID.w[:, None] * J31)
R31Z[PM - 1] = 0.0
R31Z[PM - 1, PC - 1] = MID.w[0]
J73Z = two_elements(J73)
J31Z = two_elements(J31)

CONSTS = Consts()
for tag, level in (("f", FINE), ("m", MID)):
    CONSTS.add("ky" + tag, np.concatenate(roll_coefs(level.khat)))
    kb = np.zeros(SUB)
    kb[: level.points] = level.kdiag
    kz = np.concatenate([level.kdiag, level.kdiag[1:]])
    CONSTS.add("kzb" + tag, (kz[:, None] + kb[None, :]).reshape(-1))
    ey = np.arange(LANES)
    my = np.ones((SUB, LANES))
    my[0] += ey > 0
    my[level.points - 1] += ey < LANES - 1
    mz = np.ones(level.planes)
    mz[[0, level.points - 1, -1]] = 2
    CONSTS.add("cnt" + tag, (SHIFT_MASS * mz[:, None, None] * my[None]).reshape(-1, LANES))
    CONSTS.add("mz" + tag, np.repeat(SHIFT_MASS * plane_sum(level.points), SUB))
CONSTS.add("r73", np.concatenate(roll_coefs(R73)))
CONSTS.add("j73", np.concatenate(roll_coefs(J73)))
CONSTS.add("r31", np.concatenate(roll_coefs(R31)))
CONSTS.add("j31", np.concatenate([np.pad(J31[:, p], (0, SUB - PM)) for p in range(PC)]))
CONSTS.add("iwb", 1.0 / FINE.w)

DIRS = ((-1, 0), (1, 0), (0, -1), (0, 1), (-1, -1), (-1, 1), (1, -1), (1, 1))
OPP = tuple(DIRS.index((-dx, -dz)) for dx, dz in DIRS)
COEF = 1e-13


def mix(matrix, parts):
    out = []
    for row in np.asarray(matrix):
        acc = None
        for c, v in zip(row, parts):
            if abs(c) > COEF:
                term = v if abs(c - 1.0) < COEF else float(c) * v
                acc = term if acc is None else acc + term
        out.append(acc)
    return out


def mix_even_odd(matrix, parts):
    n = len(parts)
    h = n // 2
    flipped = matrix[:h, ::-1][:, :h]
    even = mix(0.5 * (matrix[:h, :h] + flipped), [parts[i] + parts[n - 1 - i] for i in range(h)])
    odd = mix(0.5 * (matrix[:h, :h] - flipped), [parts[i] - parts[n - 1 - i] for i in range(h)])
    low = [e + o for e, o in zip(even, odd)]
    high = [e - o for e, o in zip(even, odd)]
    return low + high[::-1]


def scratch_shapes(n_node, n_dev):
    f32 = jnp.float32
    low_rows = -(-(3 * (n_dev + 1) + 1) // SUB) * SUB
    shapes = {}
    for tag, level in (("f", FINE), ("m", MID)):
        p, rows = level.points, level.rows
        for name in ("loc", "rhs", "inv", "x", "r", "d", "l"):
            shapes[name + tag] = pltpu.VMEM((p, rows, LANES), f32)
        shapes["cls" + tag] = pltpu.VMEM((3, rows, LANES), f32)
        shapes["dz" + tag] = pltpu.VMEM((rows, LANES), f32)
        shapes["rx" + tag] = pltpu.VMEM((2, 2, level.x_rows, LANES), f32)
        shapes["rz" + tag] = pltpu.VMEM((2, 2, level.z_rows, LANES), f32)
        shapes["sx" + tag] = pltpu.VMEM((2, level.x_rows, LANES), f32)
        shapes["sz" + tag] = pltpu.VMEM((2, level.z_rows, LANES), f32)
        shapes["rc" + tag] = pltpu.VMEM((2, 4, SUB, LANES), f32)
        shapes["ssem" + tag] = pltpu.SemaphoreType.DMA((8,))
        shapes["rsem" + tag] = pltpu.SemaphoreType.DMA((2, 8))
    shapes["tmpf"] = pltpu.VMEM((PF, MID.rows, LANES), f32)
    shapes["tmpm"] = pltpu.VMEM((PM, LOW.rows, LANES), f32)
    shapes["ein"] = pltpu.VMEM((PF * PF * PF * 2, LANES), f32)
    shapes["cst"] = pltpu.VMEM((CONSTS.row, LANES), f32)
    shapes["insem"] = pltpu.SemaphoreType.DMA((3,))
    shapes["eout"] = pltpu.VMEM((PF * PF * PF * 2, LANES), f32)
    shapes["outsem"] = pltpu.SemaphoreType.DMA((PF,))
    shapes["side"] = pltpu.VMEM((6, SUB, LANES), f32)
    shapes["dsrc"] = pltpu.VMEM((SUB, LANES), f32)
    shapes["dhalo"] = pltpu.VMEM((8, SUB, LANES), f32)
    shapes["dssem"] = pltpu.SemaphoreType.DMA((8,))
    shapes["drsem"] = pltpu.SemaphoreType.DMA((8,))
    shapes["da"] = pltpu.VMEM((n_dev, SUB, LANES), f32)
    shapes["db"] = pltpu.VMEM((n_node * 2 * n_dev, LANES), f32)
    shapes["ga"] = pltpu.VMEM((n_dev, SUB, LANES), f32)
    shapes["gb"] = pltpu.VMEM(((n_node + 1) * low_rows, LANES), f32)
    half = n_node // 2
    for tag in "dg":
        shapes[tag + "a_s"] = pltpu.SemaphoreType.DMA((n_dev,))
        shapes[tag + "a_r"] = pltpu.SemaphoreType.DMA((n_dev,))
        shapes[tag + "b_s"] = pltpu.SemaphoreType.DMA((half,))
        shapes[tag + "b_r"] = pltpu.SemaphoreType.DMA((half,))
        shapes[tag + "c_s"] = pltpu.SemaphoreType.DMA((half,))
        shapes[tag + "c_r"] = pltpu.SemaphoreType.DMA((half,))
    nx, nz = n_dev + 1, 2 * n_node
    for name in ("wx", "wxm", "wy", "wym", "wz", "wzm", "dg", "cx", "cr", "cq"):
        shapes["c_" + name] = pltpu.VMEM((nx, nz, 2 * LANES), f32)
    shapes["c_main"] = pltpu.VMEM((nz, LANES), f32)
    shapes["c_rest"] = pltpu.VMEM((nz, LANES), f32)
    shapes["c_p"] = pltpu.VMEM((nx, nz + 2 * SUB, 2 * LANES), f32)
    return shapes, low_rows


def make_kernel(n_node, n_dev, names, low_rows):
    half = n_node // 2
    nx, nz = n_dev + 1, 2 * n_node

    def kernel(ein_hbm, diff_hbm, cst_hbm, out_hbm, *scratch):
        s = dict(zip(names, scratch))
        node = lax.axis_index("node")
        dev = lax.axis_index("dev")
        sub = lax.broadcasted_iota(jnp.int32, (SUB, LANES), 0)
        lane = lax.broadcasted_iota(jnp.int32, (SUB, LANES), 1)
        has_lo, has_hi = dev > 0, dev < n_dev - 1

        s["dsrc"][...] = jnp.zeros_like(s["dsrc"])
        load_diff = pltpu.make_async_copy(
            diff_hbm, s["dsrc"].at[pl.ds(0, 2)], s["insem"].at[2]
        )
        load_in = pltpu.make_async_copy(ein_hbm, s["ein"], s["insem"].at[0])
        load_cst = pltpu.make_async_copy(cst_hbm, s["cst"], s["insem"].at[1])
        load_diff.start()
        load_in.start()
        load_cst.start()

        def const(name, index=None):
            row, size = CONSTS.at[name]
            if index is None:
                return s["cst"][row : row + size, :]
            return s["cst"][row + SUB * index : row + SUB * index + SUB, :]

        def guarded(dx, fn):
            if dx == 0:
                fn()
            else:
                pl.when(has_lo if dx < 0 else has_hi)(fn)

        def neighbour(dx, dz):
            return (lax.rem(node + dz + n_node, n_node), dev + dx)

        sibling = (node + 1 - 2 * lax.rem(node, 2), dev)

        def same_core(k):
            return lax.rem(node + 2 * k, n_node)

        for tag in "fm":
            for name in ("rx", "rz", "rc"):
                s[name + tag][...] = jnp.zeros_like(s[name + tag])
        s["dhalo"][...] = jnp.zeros_like(s["dhalo"])

        barrier = pltpu.get_barrier_semaphore()

        def greet(target):
            pl.semaphore_signal(barrier, inc=1, device_id=target, device_id_type=MESH)

        for dx, dz in DIRS:
            guarded(dx, lambda dx=dx, dz=dz: greet(neighbour(dx, dz)))
        far = lambda k: lax.rem(dev + k, n_dev)

        def greet_far(k, _):
            greet((node, lax.rem(dev + k, n_dev)))
            return 0

        def greet_cores(k, _):
            greet((same_core(k), dev))
            return 0

        lax.fori_loop(1, n_dev, greet_far, 0)
        lax.fori_loop(1, half, greet_cores, 0)
        ends = has_lo.astype(jnp.int32) + has_hi.astype(jnp.int32)

        def wait_barrier():
            pl.semaphore_wait(barrier, n_dev - 1 + half - 1 + 2 + 3 * ends)

        def face_copy(tag, par, i):
            level = FINE if tag == "f" else MID
            dx, dz = DIRS[i]
            j = OPP[i]
            if dz == 0:
                src, dst = s["sx" + tag].at[i], s["rx" + tag].at[par, j]
            elif dx == 0:
                src, dst = s["sz" + tag].at[i - 2], s["rz" + tag].at[par, j - 2]
            else:
                a = 0 if dx < 0 else level.points - 1
                zrow = pl.ds(0 if dz < 0 else level.rows - SUB, SUB)
                src, dst = s["loc" + tag].at[a, zrow], s["rc" + tag].at[par, j - 4]
            return pltpu.make_async_remote_copy(
                src_ref=src,
                dst_ref=dst,
                send_sem=s["ssem" + tag].at[i],
                recv_sem=s["rsem" + tag].at[par, j],
                device_id=neighbour(dx, dz),
                device_id_type=MESH,
            )

        def halo_copy(i):
            return pltpu.make_async_remote_copy(
                src_ref=s["dsrc"],
                dst_ref=s["dhalo"].at[OPP[i]],
                send_sem=s["dssem"].at[i],
                recv_sem=s["drsem"].at[OPP[i]],
                device_id=neighbour(*DIRS[i]),
                device_id_type=MESH,
            )

        def start_some(make, which):
            for i in which:
                guarded(DIRS[i][0], lambda i=i: make(i).start())

        def wait_some(make, which):
            for i in which:
                guarded(DIRS[i][0], lambda i=i: make(i).wait_send())
            for i in which:
                guarded(DIRS[OPP[i]][0], lambda i=i: make(i).wait_recv())

        X_DIRS, Z_DIRS, EDGE_DIRS = (0, 1), (2, 3), (4, 5, 6, 7)
        parity = {"f": 0, "m": 0}

        def start_faces(tag, which):
            start_some(lambda i: face_copy(tag, parity[tag], i), which)

        def pack(tag, parts):
            if tag == "f":
                return parts
            h = -(-len(parts) // 2)
            return [
                parts[i] + pltpu.roll(parts[i + h], PM, 0) if i + h < len(parts) else parts[i]
                for i in range(h)
            ]

        def unpack(tag, v, count):
            parts = [v[SUB * i : SUB * i + SUB] for i in range(v.shape[0] // SUB)]
            if tag == "f":
                return parts
            out = parts + [pltpu.roll(t, PM, 0) for t in parts]
            return [jnp.where(sub < PM, t, 0.0) for t in out[:count]]

        def put(ref, index, parts):
            for i, t in enumerate(parts):
                ref[index, SUB * i : SUB * i + SUB, :] = t

        def add_faces(tag, edges):
            level = FINE if tag == "f" else MID
            par = parity[tag]
            parity[tag] = 1 - par
            which = X_DIRS + Z_DIRS + (EDGE_DIRS if edges else ())
            wait_some(lambda i: face_copy(tag, par, i), which)
            buf, rx, rz, rc = (s[n + tag] for n in ("l", "rx", "rz", "rc"))
            last, top = level.points - 1, level.rows - SUB
            for side, a in ((0, 0), (1, last)):
                for z, t in enumerate(unpack(tag, rx[par, side], level.planes)):
                    buf[a, SUB * z : SUB * z + SUB, :] += t
            for side, row in ((0, 0), (1, top)):
                for a, t in enumerate(unpack(tag, rz[par, side], level.points)):
                    buf[a, row : row + SUB, :] += t
            if edges:
                for k, (a, row) in enumerate(((0, 0), (0, top), (last, 0), (last, top))):
                    buf[a, row : row + SUB, :] += rc[par, k]

        def sum_y(tag, a, first=0, count=None):
            level = FINE if tag == "f" else MID
            n = level.planes if count is None else count
            buf = s["l" + tag]
            rows_lo = pl.ds(SUB * first, n, stride=SUB)
            rows_hi = pl.ds(SUB * first + level.points - 1, n, stride=SUB)
            lo, hi = buf[a, rows_lo, :], buf[a, rows_hi, :]
            at = lax.broadcasted_iota(jnp.int32, (n, LANES), 1)
            buf[a, rows_lo, :] = lo + jnp.where(at > 0, pltpu.roll(hi, 1, 1), 0.0)
            buf[a, rows_hi, :] = hi + jnp.where(
                at < LANES - 1, pltpu.roll(lo, LANES - 1, 1), 0.0
            )

        def sum_y_planes(tag, row):
            p = (FINE if tag == "f" else MID).points
            sel = (slice(1, p - 1), slice(row, row + SUB))
            t = s["l" + tag][sel]
            up = pltpu.roll(pltpu.roll(t, 1, 2), SUB - p + 1, 1)
            down = pltpu.roll(pltpu.roll(t, LANES - 1, 2), p - 1, 1)
            t = t + jnp.where((sub == 0) & (lane > 0), up, 0.0)
            t = t + jnp.where((sub == p - 1) & (lane < LANES - 1), down, 0.0)
            s["l" + tag][sel] = t

        def gather_a(tag, k):
            buf = s[tag + "a"]
            return pltpu.make_async_remote_copy(
                src_ref=buf.at[dev],
                dst_ref=buf.at[dev],
                send_sem=s[tag + "a_s"].at[k],
                recv_sem=s[tag + "a_r"].at[k],
                device_id=(node, far(k)),
                device_id_type=MESH,
            )

        block = {"d": 2 * n_dev, "g": low_rows}
        base = {"d": 0, "g": low_rows}

        def slot(tag, index):
            size = block[tag]
            return s[tag + "b"].at[pl.ds(pl.multiple_of(base[tag] + index * size, size), size)]

        def gather_b(tag, k):
            return pltpu.make_async_remote_copy(
                src_ref=slot(tag, node),
                dst_ref=slot(tag, node),
                send_sem=s[tag + "b_s"].at[k],
                recv_sem=s[tag + "b_r"].at[k],
                device_id=(same_core(k), dev),
                device_id_type=MESH,
            )

        def gather_c(tag, k):
            index = lax.rem(node - 2 * k + n_node, n_node)
            return pltpu.make_async_remote_copy(
                src_ref=slot(tag, index),
                dst_ref=slot(tag, index),
                send_sem=s[tag + "c_s"].at[k],
                recv_sem=s[tag + "c_r"].at[k],
                device_id=sibling,
                device_id_type=MESH,
            )

        def loop(lower, upper, fn):
            def step(k, _):
                fn(k)
                return 0

            lax.fori_loop(lower, upper, step, 0)

        def start_a(tag):
            loop(1, n_dev, lambda k: gather_a(tag, k).start())

        def wait_a(tag):
            loop(1, n_dev, lambda k: gather_a(tag, k).wait())

        def start_b(tag):
            loop(1, half, lambda k: gather_b(tag, k).start())
            gather_c(tag, 0).start()

        def forward_b(tag):
            def one(k):
                gather_b(tag, k).wait_recv()
                gather_c(tag, k).start()

            loop(1, half, one)

        def wait_b(tag):
            loop(1, half, lambda k: gather_b(tag, k).wait_send())
            loop(0, half, lambda k: gather_c(tag, k).wait())

        def along_y(tag, v):
            p = (FINE if tag == "f" else MID).points
            acc = const("ky" + tag, 0) * v
            for shift in range(1, SUB):
                if p == PF or shift < p or shift > SUB - p:
                    acc = acc + const("ky" + tag, shift) * pltpu.roll(v, shift, 1)
            return acc

        def along_z(tag, v):
            level = FINE if tag == "f" else MID
            n, p = level.planes, level.points
            parts = [v[SUB * i : SUB * i + SUB] for i in range(n)]
            low = mix_even_odd(level.khat, parts[:p])
            high = mix_even_odd(level.khat, parts[p - 1 :])
            first = s["dz" + tag][0:SUB, :]
            second = s["dz" + tag][level.rows - SUB : level.rows, :]
            out = [first * t for t in low[: p - 1]]
            out.append(first * low[p - 1] + second * high[0])
            out += [second * t for t in high[1:]]
            return out, low[0], high[-1]

        def faces(tag, name):
            level = FINE if tag == "f" else MID
            n, p, top = level.planes, level.points, level.rows - SUB
            src, dst, dz = s[name + tag], s["l" + tag], s["dz" + tag]
            mass_row, _ = CONSTS.at["mz" + tag]
            has = (has_lo.astype(jnp.float32), has_hi.astype(jnp.float32))
            ends = (0, p - 1)
            even_row = 0.5 * (level.khat[0:1] + level.khat[0:1, ::-1])[:, : p // 2]
            odd_row = 0.5 * (level.khat[0:1] - level.khat[0:1, ::-1])[:, : p // 2]
            x_edge, z_edge = {}, {}
            chunk = 5 if tag == "f" else n
            for z0 in range(0, n, chunk):
                rows = slice(SUB * z0, SUB * (z0 + chunk))
                v = [src[a, rows, :] for a in range(p)]
                even = mix(even_row, [v[i] + v[p - 1 - i] for i in range(p // 2)])[0]
                odd = mix(odd_row, [v[i] - v[p - 1 - i] for i in range(p // 2)])[0]
                for f, xt in ((0, even + odd), (1, even - odd)):
                    if z0 == 0:
                        x_edge[f, 0] = xt[0:SUB]
                    if z0 + chunk == n:
                        x_edge[f, 1] = xt[-SUB:]
                    u = v[ends[f]]
                    yt = along_y(tag, u.reshape(chunk, SUB, LANES)).reshape(chunk * SUB, LANES)
                    mass = s["cst"][mass_row + SUB * z0 : mass_row + SUB * (z0 + chunk), :]
                    dst[ends[f], rows, :] = dz[rows, :] * (xt + yt) + mass * u
            for f, a in enumerate(ends):
                out, z_edge[f, 0], z_edge[f, 1] = along_z(tag, src[a])
                out = [t + dst[a, SUB * z : SUB * z + SUB, :] for z, t in enumerate(out)]
                put(dst, a, out)
                out[0] = out[0] + s["side"][4] * x_edge[f, 0]
                out[-1] = out[-1] + s["side"][5] * x_edge[f, 1]
                put(s["sx" + tag], f, pack(tag, out))
            start_faces(tag, X_DIRS)
            for side, row in ((0, 0), (1, top)):
                rows = slice(row, row + SUB)
                v = src[:, rows, :]
                yt = along_y(tag, v)
                xt = mix_even_odd(level.khat, [v[a] for a in range(p)])
                plane0 = 0 if side == 0 else p - 1
                zt = mix(
                    level.khat[p - 1 : p] if side else level.khat[0:1],
                    [
                        src[1 : p - 1, SUB * (plane0 + c) : SUB * (plane0 + c) + SUB, :]
                        for c in range(p)
                    ],
                )[0]
                weight = dz[rows, :]
                out = [None] * p
                for a in range(1, p - 1):
                    out[a] = weight * (xt[a] + yt[a] + zt[a - 1]) + SHIFT_MASS * v[a]
                    dst[a, rows, :] = out[a]
                for f, a in enumerate(ends):
                    out[a] = (
                        dst[a, rows, :]
                        + s["side"][2 * f + side] * (z_edge[f, side] + yt[a])
                        + (SHIFT_MASS * has[f]) * v[a]
                    )
                put(s["sz" + tag], side, pack(tag, out))
            start_faces(tag, Z_DIRS)

        def interior(tag, name, after=None):
            level = FINE if tag == "f" else MID
            n, p = level.planes, level.points
            src, dst = s[name + tag], s["l" + tag]

            def plane(z):
                rows = pl.ds(pl.multiple_of(z * SUB, SUB), SUB)
                v = src[:, rows, :]
                acc = along_y(tag, v[1 : p - 1])
                along_x = mix_even_odd(level.khat, [v[a] for a in range(p)])
                weight = s["dz" + tag][rows, :]
                mass = jnp.where(z == p - 1, 2.0 * SHIFT_MASS, SHIFT_MASS)
                for a in range(1, p - 1):
                    dst[a, rows, :] = weight * (acc[a - 1] + along_x[a]) + mass * v[a]

            loop(1, n - 1, plane)

            def line(a):
                out, _, _ = along_z(tag, src[a])
                for i in range(1, n - 1):
                    dst[a, SUB * i : SUB * i + SUB, :] += out[i]
                if after is not None:
                    after(a)

            loop(1, p - 1, line)

        def apply(tag, name):
            level = FINE if tag == "f" else MID
            n, p = level.planes, level.points
            src, dst = s[name + tag], s["l" + tag]

            def plane(z):
                rows = pl.ds(pl.multiple_of(z * SUB, SUB), SUB)
                v = src[:, rows, :]
                acc = along_y(tag, v)
                along_x = mix_even_odd(level.khat, [v[a] for a in range(p)])
                weight = s["dz" + tag][rows, :]
                mass = jnp.where(z == p - 1, 2.0 * SHIFT_MASS, SHIFT_MASS)
                for a in range(p):
                    dst[a, rows, :] = weight * (acc[a] + along_x[a]) + mass * v[a]

            loop(0, n, plane)

            def line(a):
                out, _, _ = along_z(tag, src[a])
                for i in range(n):
                    dst[a, SUB * i : SUB * i + SUB, :] += out[i]

            loop(0, p, line)

        def update(tag, kind, c1=0.0, c2=0.0, last=False, residual="r"):
            level = FINE if tag == "f" else MID
            c = float(1.0 / level.theta)
            l, rhs, inv, x, r, d = (s[k + tag] for k in ("l", "rhs", "inv", "x", "r", "d"))
            old = s[residual + tag]

            def on(*sel):
                if kind == "zero":
                    res = l[sel]
                    rhs[sel] = res
                    upd = c * inv[sel] * res
                    d[sel] = upd
                    x[sel] = upd
                elif kind == "first":
                    res = rhs[sel] - l[sel]
                    r[sel] = res
                    upd = c * inv[sel] * res
                    d[sel] = upd
                    x[sel] = x[sel] + upd
                else:
                    res = old[sel] - l[sel]
                    upd = c1 * d[sel] + c2 * inv[sel] * res
                    if not last:
                        r[sel] = res
                        d[sel] = upd
                    x[sel] = x[sel] + upd

            return on

        def inner_update(tag, on):
            level = FINE if tag == "f" else MID

            def one(a):
                sum_y(tag, a, 1, level.planes - 2)
                on(a, slice(SUB, level.rows - SUB))

            return one

        def face_update(tag, on, edges=False):
            level = FINE if tag == "f" else MID
            add_faces(tag, edges)
            for a in (0, level.points - 1):
                sum_y(tag, a)
                on(a, slice(0, level.rows))
            for row in (0, level.rows - SUB):
                sum_y_planes(tag, row)
                on(slice(1, level.points - 1), slice(row, row + SUB))

        def raw_round(tag, on, before_inner, before_faces):
            level = FINE if tag == "f" else MID
            buf, last, top = s["l" + tag], level.points - 1, level.rows - SUB
            start_faces(tag, EDGE_DIRS)
            for f, a in ((0, 0), (1, last)):
                put(
                    s["sx" + tag],
                    f,
                    pack(tag, [buf[a, SUB * z : SUB * z + SUB, :] for z in range(level.planes)]),
                )
            start_faces(tag, X_DIRS)
            for side, row in ((0, 0), (1, top)):
                put(
                    s["sz" + tag],
                    side,
                    pack(tag, [buf[a, row : row + SUB, :] for a in range(level.points)]),
                )
            start_faces(tag, Z_DIRS)
            before_inner()
            loop(1, last, inner_update(tag, on))
            before_faces()
            face_update(tag, on, True)

        def steps(tag, count, residual, between):
            coefs = (FINE if tag == "f" else MID).steps(count)
            for index, (c1, c2) in enumerate(coefs):
                on = update(tag, "next", c1, c2, index == count - 2, residual)
                residual = "r"
                faces(tag, "d")
                interior(tag, "d", inner_update(tag, on))
                between[index]()
                face_update(tag, on)

        ones = [has_lo.astype(jnp.float32), 1.0, has_hi.astype(jnp.float32)]
        copies = [1.0 + ones[0], 1.0, 1.0 + ones[2]]
        levels = (("f", FINE), ("m", MID))

        def spread_row(row):
            return jnp.broadcast_to(row, (SUB, LANES))

        def patch(dx):
            at = lambda dz: s["dhalo"].at[DIRS.index((dx, dz))]
            mid = s["dsrc"] if dx == 0 else at(0)
            rows = [at(-1)[1:2, :], mid[0:1, :], mid[1:2, :], at(1)[0:1, :]]
            return [spread_row(row) for row in rows]

        def kinds_of(q):
            return [q[0] + q[1], q[1], q[1] + q[2], q[2], q[2] + q[3]]

        def kind_of(z, p):
            return {0: 0, p - 1: 2, 2 * p - 2: 4}.get(z, 1 if z < p else 3)

        def nodal(k, p):
            lo = k + jnp.where(lane > 0, pltpu.roll(k, 1, 1), 0.0)
            hi = k + jnp.where(lane < LANES - 1, pltpu.roll(k, LANES - 1, 1), 0.0)
            return jnp.where(sub == 0, lo, jnp.where(sub == p - 1, hi, k))

        def set_inverse(tag, level, a, xc, rows):
            row_k, _ = CONSTS.at["kzb" + tag]
            row_c, _ = CONSTS.at["cnt" + tag]
            kzb = s["cst"][row_k + rows.start : row_k + rows.stop, :]
            cnt = s["cst"][row_c + rows.start : row_c + rows.stop, :]
            diag = (float(level.kdiag[a]) + kzb) * s["cls" + tag][xc, rows, :]
            s["inv" + tag][a, rows, :] = 1.0 / (diag + copies[xc] * cnt)

        def diagonals_inside():
            first, second = spread_row(s["dsrc"][0:1, :]), spread_row(s["dsrc"][1:2, :])
            kinds = [first, first, first + second, second, second]
            for tag, level in levels:
                p = level.points
                full = [nodal(k, p) for k in kinds]
                for z in range(level.planes):
                    rows = slice(SUB * z, SUB * z + SUB)
                    s["dz" + tag][rows, :] = kinds[kind_of(z, p)]
                    s["cls" + tag][1, rows, :] = full[kind_of(z, p)]
                for a in range(1, p - 1):
                    set_inverse(tag, level, a, 1, slice(SUB, level.rows - SUB))

        def diagonals_faces():
            q = [patch(-1), patch(0), patch(1)]
            for side in range(2):
                s["side"][side] = q[0][1 + side]
                s["side"][2 + side] = q[2][1 + side]
                s["side"][4 + side] = q[1][3 * side]
            xs = [[u + v for u, v in zip(q[0], q[1])], q[1], [u + v for u, v in zip(q[1], q[2])]]
            for xc in range(3):
                kinds = kinds_of(xs[xc])
                for tag, level in levels:
                    p = level.points
                    full = [
                        None if xc == 1 and i in (1, 2, 3) else nodal(k, p)
                        for i, k in enumerate(kinds)
                    ]
                    for z in range(level.planes):
                        value = full[kind_of(z, p)]
                        if value is not None:
                            s["cls" + tag][xc, SUB * z : SUB * z + SUB, :] = value
            for tag, level in levels:
                p, n = level.points, level.rows
                set_inverse(tag, level, 0, 0, slice(0, n))
                set_inverse(tag, level, p - 1, 2, slice(0, n))
                for a in range(1, p - 1):
                    set_inverse(tag, level, a, 1, slice(0, SUB))
                    set_inverse(tag, level, a, 1, slice(n - SUB, n))

        def restrict_fine():
            def line(a):
                res = s["locf"][a] - s["lf"][a]
                parts = [res[SUB * i : SUB * i + SUB] for i in range(FINE.planes)]
                for i, t in enumerate(mix(R73Z.T, parts)):
                    s["tmpf"][a, SUB * i : SUB * i + SUB, :] = t

            loop(0, PF, line)

            def plane(z):
                rows = pl.ds(pl.multiple_of(z * SUB, SUB), SUB)
                v = s["tmpf"][:, rows, :]
                t = jnp.stack(mix(R73, [v[a] for a in range(PF)]))
                acc = const("r73", 0) * t
                for shift in range(1, SUB):
                    acc = acc + const("r73", shift) * pltpu.roll(t, shift, 1)
                s["locm"][:, rows, :] = acc
                s["lm"][:, rows, :] = acc

            loop(0, MID.planes, plane)

        def prolong_fine():
            def plane(z):
                rows = pl.ds(pl.multiple_of(z * SUB, SUB), SUB)
                v = s["xm"][:, rows, :]
                acc = const("j73", 0) * v
                for shift in range(1, SUB):
                    acc = acc + const("j73", shift) * pltpu.roll(v, shift, 1)
                for a, t in enumerate(mix(J73, [acc[i] for i in range(PM)])):
                    s["tmpf"][a, rows, :] = t

            loop(0, MID.planes, plane)

            def line(a):
                v = s["tmpf"][a]
                parts = [v[SUB * i : SUB * i + SUB] for i in range(MID.planes)]
                for i, t in enumerate(mix(J73Z, parts)):
                    s["xf"][a, SUB * i : SUB * i + SUB, :] += t

            loop(0, PF, line)

        def restrict_mid():
            for a in range(PM):
                res = s["locm"][a] - s["lm"][a]
                parts = [res[SUB * i : SUB * i + SUB] for i in range(MID.planes)]
                for i, t in enumerate(mix(R31Z.T, parts)):
                    s["tmpm"][a, SUB * i : SUB * i + SUB, :] = t
            spare = jnp.zeros((SUB, LANES), jnp.float32)
            for z in range(3):
                v = s["tmpm"][:, SUB * z : SUB * z + SUB, :]
                for a, t in enumerate(mix(R31, [v[i] for i in range(PM)])):
                    acc = const("r31", 0) * t
                    for shift in (1, 5, 6, 7):
                        acc = acc + const("r31", shift) * pltpu.roll(t, shift, 0)
                    up = pltpu.roll(pltpu.roll(acc, 1, 1), SUB - 1, 0)
                    node_row = acc + jnp.where(lane > 0, up, 0.0)
                    s["ga"][dev, 3 * a + z : 3 * a + z + 1, :] = node_row[0:1, :]
                    spare = spare + jnp.where(lane == z * nx + dev + a, up[0:1, 0:1], 0.0)
            s["ga"][dev, 6:7, :] = spare[0:1, :]
            s["ga"][dev, 7:8, :] = jnp.zeros((1, LANES), jnp.float32)

        def sum_x_low():
            flat = s["ga"]
            g = jnp.zeros((low_rows, LANES), jnp.float32)
            pad = lambda rows, before: jnp.pad(
                rows, ((before, low_rows - before - rows.shape[0]), (0, 0))
            )
            mine = s["gb"].at[
                pl.ds(pl.multiple_of(low_rows + node * low_rows, low_rows), low_rows)
            ]
            mine[...] = g
            for z in range(3):
                mine[z * nx : z * nx + n_dev, :] = flat[:, z, :]
                mine[z * nx + 1 : z * nx + nx, :] += flat[:, 3 + z, :]
            mine[3 * nx : 3 * nx + 1, :] = jnp.sum(flat[:, 6, :], axis=0, keepdims=True)

        def wide(rows):
            return jnp.concatenate([rows, jnp.zeros_like(rows)], axis=1)

        def low_weights():
            up_y = lambda v: pltpu.roll(v, 1, 1)
            up_z = lambda v: pltpu.roll(v, 1, 0)
            elem = lambda x: s["db"][pl.ds(x, nz, stride=n_dev), :]
            zero = jnp.zeros((nz, 2 * LANES), jnp.float32)
            lanes = lax.broadcasted_iota(jnp.int32, (nz, 2 * LANES), 1)
            inside = (lanes <= LANES).astype(jnp.float32)
            y_copies = (
                inside + ((lanes > 0) & (lanes < LANES)).astype(jnp.float32)
            )
            for x in range(nx):
                lo = wide(elem(x - 1)) if x > 0 else zero
                hi = wide(elem(x)) if x < n_dev else zero
                both = lo + hi
                wy = 0.5 * (both + up_z(both))
                wz = 0.5 * (both + up_y(both))
                s["c_wy"][x] = wy
                s["c_wym"][x] = up_y(wy)
                s["c_wz"][x] = wz
                s["c_wzm"][x] = up_z(wz)
                hz = hi + up_z(hi)
                wx = 0.5 * (hz + up_y(hz))
                s["c_wx"][x] = wx
                wxm = s["c_wx"][x - 1] if x > 0 else zero
                x_copies = 1.0 if x in (0, n_dev) else 2.0
                s["c_dg"][x] = (
                    wx + wxm + wy + s["c_wym"][x] + wz + s["c_wzm"][x]
                    + 2.0 * SHIFT_MASS * x_copies * y_copies
                )

        def low_rhs():
            buf = s["gb"]
            buf[0:low_rows, :] = buf[n_node * low_rows : (n_node + 1) * low_rows, :]
            own = lambda row: buf[pl.ds(low_rows + row, n_node, stride=low_rows), :]
            before = lambda row: buf[pl.ds(row, n_node, stride=low_rows), :]
            at = lax.broadcasted_iota(jnp.int32, (n_node, LANES), 1)
            spare, spare_before = own(3 * nx), before(3 * nx)

            def pick(rows, lane_index):
                moved = rows if lane_index == 0 else pltpu.roll(rows, LANES - lane_index, 1)
                return jnp.where(at == 0, moved, 0.0)

            even, odd = pl.ds(0, n_node, stride=2), pl.ds(1, n_node, stride=2)
            left, right = pl.ds(0, LANES), pl.ds(LANES, LANES)
            res, main, rest = s["c_cr"], s["c_main"], s["c_rest"]
            for x in range(nx):
                main[even, :] = own(x) + before(2 * nx + x)
                main[odd, :] = own(nx + x)
                rest[even, :] = pick(spare, x) + pick(spare_before, 2 * nx + x)
                rest[odd, :] = pick(spare, nx + x)
                res[x, :, left] = main[...]
                res[x, :, right] = rest[...]

        def fold(v):
            parts = [v[i : i + SUB] for i in range(0, v.shape[0], SUB)]
            while len(parts) > 1:
                parts = [u + w for u, w in zip(parts[::2], parts[1::2])] + (
                    [parts[-1]] if len(parts) % 2 else []
                )
            return parts[0][:, :LANES] + parts[0][:, LANES:]

        def total(v):
            return jnp.sum(v, axis=(0, 1), keepdims=True)

        def set_direction(x, value):
            p = s["c_p"]
            p[x, SUB : SUB + nz, :] = value
            p[x, 0:SUB, :] = value[nz - SUB : nz]
            p[x, SUB + nz : 2 * SUB + nz, :] = value[0:SUB]

        def coarse_solve():
            p, q, res, sol = s["c_p"], s["c_cq"], s["c_cr"], s["c_cx"]
            wide_lanes = 2 * LANES
            here = pl.ds(SUB, nz)
            norm = jnp.zeros((SUB, LANES), jnp.float32)
            for x in range(nx):
                v = res[x]
                set_direction(x, v)
                sol[x] = jnp.zeros_like(v)
                norm = norm + fold(v * v)

            def iteration(_, now):
                dot = jnp.zeros((SUB, LANES), jnp.float32)
                for x in range(nx):
                    v = p[x, here, :]
                    out = s["c_dg"][x] * v
                    if x > 0:
                        out = out - s["c_wx"][x - 1] * p[x - 1, here, :]
                    if x < nx - 1:
                        out = out - s["c_wx"][x] * p[x + 1, here, :]
                    out = out - s["c_wy"][x] * pltpu.roll(v, wide_lanes - 1, 1)
                    out = out - s["c_wym"][x] * pltpu.roll(v, 1, 1)
                    out = out - s["c_wz"][x] * p[x, SUB + 1 : SUB + 1 + nz, :]
                    out = out - s["c_wzm"][x] * p[x, SUB - 1 : SUB - 1 + nz, :]
                    q[x] = out
                    dot = dot + fold(v * out)
                alpha = now / total(dot)
                norm = jnp.zeros((SUB, LANES), jnp.float32)
                for x in range(nx):
                    sol[x] += alpha * p[x, here, :]
                    v = res[x] - alpha * q[x]
                    res[x] = v
                    norm = norm + fold(v * v)
                new = total(norm)
                beta = new / now
                for x in range(nx):
                    set_direction(x, res[x] + beta * p[x, here, :])
                return new

            lax.fori_loop(0, COARSE_ITERS, iteration, total(norm))

        def add_low():
            p, n = PM, MID.planes
            h = float((MID.khat @ J31)[0, 0])
            spread = {}
            for i in range(4):
                for k in range(5):
                    if i in (0, 3) and k in (0, 4):
                        continue
                    x = jnp.clip(dev + i - 1, 0, n_dev)
                    z = lax.rem(2 * node + k - 1 + nz, nz)
                    row = s["c_cx"][x, pl.ds(z, 1), :]
                    row = jnp.broadcast_to(row, (SUB, 2 * LANES))
                    low = row[:, :LANES]
                    high = pltpu.roll(row, 2 * LANES - 1, 1)[:, :LANES]
                    spread[i, k] = const("j31", 0) * low + const("j31", 1) * high
            left = mix(J31Z, [spread[0, k] for k in (1, 2, 3)])
            right = mix(J31Z, [spread[3, k] for k in (1, 2, 3)])
            inner = [
                mix(J31, [spread[1, k], spread[2, k]]) for k in range(5)
            ]
            q = [patch(-1), patch(0), patch(1)]
            xs = [[u + v for u, v in zip(q[0], q[1])], q[1], [u + v for u, v in zip(q[1], q[2])]]
            along_x = [kinds_of(v) for v in q]
            lines = [mix(J31Z, [inner[k][a] for k in (1, 2, 3)]) for a in range(p)]
            for a in range(p):
                xc = 0 if a == 0 else 2 if a == p - 1 else 1
                w, u = xs[xc], lines[a]
                kinds = kinds_of(w)
                ends = (0, p - 1, n - 1)
                slope = [u[0] - inner[0][a], u[p - 1] - u[0], u[n - 1] - u[p - 1], inner[4][a] - u[n - 1]]
                flow = [v * t for v, t in zip(w, slope)]
                for z in range(n):
                    rows = slice(SUB * z, SUB * z + SUB)
                    kind = kind_of(z, p)
                    copies_z = 2.0 if z in ends else 1.0
                    out = kinds[kind] * along_y("m", u[z][None])[0]
                    out = out + (SHIFT_MASS * copies_z * copies[xc]) * u[z]
                    if z in ends:
                        k = ends.index(z)
                        out = out + h * (flow[k] - flow[k + 1])
                    if a == 0:
                        out = out + h * (
                            along_x[0][kind] * (u[z] - left[z])
                            + along_x[1][kind] * (u[z] - lines[p - 1][z])
                        )
                    if a == p - 1:
                        out = out + h * (
                            along_x[1][kind] * (u[z] - lines[0][z])
                            + along_x[2][kind] * (u[z] - right[z])
                        )
                    s["lm"][a, rows, :] += out
                    s["xm"][a, rows, :] += u[z]

        nothing = lambda: None
        load_diff.wait()
        s["da"][dev] = s["dsrc"][...]
        wait_barrier()
        start_some(halo_copy, range(8))
        load_cst.wait()
        load_in.wait()
        wz = np.concatenate([FINE.w, FINE.w[1:]])

        def load_line(a):
            planes = []
            for e in range(2):
                for c in range(PF):
                    start = a * (PF * PF * 2) + 2 * c + e
                    planes.append(s["ein"][pl.ds(start, SUB, stride=2 * PF), :])
            merged = planes[: PF - 1] + [planes[PF - 1] + planes[PF]] + planes[PF + 1 :]
            scale = const("iwb") * wa_inverse(a)
            for z, v in enumerate(merged):
                t = scale * v * float(1.0 / wz[z])
                s["locf"][a, SUB * z : SUB * z + SUB, :] = t
                s["lf"][a, SUB * z : SUB * z + SUB, :] = t

        def wa_inverse(a):
            value = jnp.float32(1.0 / FINE.w[0])
            for i in range(1, PF // 2):
                value = jnp.where((a == i) | (a == PF - 1 - i), 1.0 / FINE.w[i], value)
            return value

        loop(0, PF, load_line)

        def halo_done():
            start_a("d")
            wait_some(halo_copy, range(8))
            diagonals_faces()

        def diff_stage_b():
            wait_a("d")
            mine = slot("d", node)
            for e in range(2):
                mine[e * n_dev : (e + 1) * n_dev, :] = s["da"][:, e, :]
            start_b("d")

        raw_round("f", update("f", "zero"), diagonals_inside, halo_done)
        steps("f", SMOOTH_FINE, "rhs", [diff_stage_b, lambda: forward_b("d")])
        apply("f", "x")
        restrict_fine()

        def weights():
            wait_b("d")
            low_weights()

        raw_round("m", update("m", "zero"), nothing, weights)
        steps("m", SMOOTH_MID, "rhs", [nothing, nothing])
        faces("m", "x")
        interior("m", "x")
        restrict_mid()
        start_a("g")
        add_faces("m", False)
        wait_a("g")
        sum_x_low()
        start_b("g")
        forward_b("g")
        wait_b("g")
        low_rhs()
        coarse_solve()
        add_low()
        first = update("m", "first")

        def first_mid(a):
            sum_y("m", a)
            first(a, slice(0, MID.rows))

        loop(0, PM, first_mid)
        steps("m", SMOOTH_MID, "r", [nothing, nothing])
        prolong_fine()
        first = update("f", "first")
        faces("f", "x")
        interior("f", "x", inner_update("f", first))
        face_update("f", first)
        steps("f", SMOOTH_FINE, "r", [nothing, nothing])

        chunk = PF * PF * 2

        def out_copy(a):
            rows = pl.ds(pl.multiple_of(a * chunk, chunk), chunk)
            return pltpu.make_async_copy(
                s["eout"].at[rows], out_hbm.at[rows], s["outsem"].at[a]
            )

        def store_line(a):
            for e in range(2):
                for c in range(PF):
                    z = e * (PF - 1) + c
                    start = a * chunk + 2 * c + e
                    s["eout"][pl.ds(start, SUB, stride=2 * PF), :] = s["xf"][
                        a, SUB * z : SUB * z + SUB, :
                    ]
            out_copy(a).start()

        loop(0, PF, store_line)
        loop(0, PF, lambda a: out_copy(a).wait())

    return kernel


def solution(mesh):
    n_node, n_dev = mesh.shape["node"], mesh.shape["dev"]
    shapes, low_rows = scratch_shapes(n_node, n_dev)
    kernel = make_kernel(n_node, n_dev, list(shapes), low_rows)
    rows = PF * PF * PF * 2

    def local(element_load, diffusivity):
        out = pl.pallas_call(
            kernel,
            out_shape=jax.ShapeDtypeStruct((rows, LANES), jnp.float32),
            in_specs=[pl.BlockSpec(memory_space=pltpu.HBM)] * 3,
            out_specs=pl.BlockSpec(memory_space=pltpu.HBM),
            scratch_shapes=list(shapes.values()),
            compiler_params=pltpu.CompilerParams(
                collective_id=0, has_side_effects=True, vmem_limit_bytes=48 * 1024 * 1024
            ),
        )(
            element_load.reshape(rows, LANES),
            diffusivity.reshape(2, LANES),
            jnp.asarray(CONSTS.array()),
        )
        return out.reshape(element_load.shape)

    return jax.shard_map(
        local,
        mesh=mesh,
        in_specs=(P(None, None, None, "dev", "node", None), P("dev", "node", None)),
        out_specs=P(None, None, None, "dev", "node", None),
        check_vma=False,
    )
```

profile of v0, /device:TPU:32, one launch (start us, length us, event | category | flops | bytes accessed | tf_op | source)
XLA Modules:
  0.0 84.3 jit_solution(8700644941150199484)
XLA Ops:
  0.0 0.0 copy-start.2
  0.0 0.7 copy-done.2
  0.7 0.0 copy-start
  0.7 1.0 %copy-done = f32[8,8,8,1,2,128]{5,4,3,2,1,0:T(2,128)S(1)} copy-done((f32[8,8,8,1,2,128]{5,4,3,2,1,0:T(2,128)S(1)}, f32[8,8,8,1,2,128]{5,4,3,2,1,0:T(2,128)}, u32[]{:S(2)}) %copy-start) | copy-done | bytes 524312
  1.7 0.0 copy-start.1
  1.7 1.0 %copy-done.1 = f32[872,128]{1,0:T(8,128)S(1)} copy-done((f32[872,128]{1,0:T(8,128)S(1)}, f32[872,128]{1,0:T(8,128)}, u32[]{:S(2)}) %copy-start.1) | copy-done | bytes 446488
  2.7 80.8 %shard_map.37 = f32[1024,128]{1,0:T(8,128)S(1)} custom-call(f32[1024,128]{1,0:T(8,128)S(1)} %bitcast.6, f32[2,128]{1,0:T(2,128)S(1)} %bitcast.7, f32[872,128]{1,0:T(8,128)S(1)} %copy-done.1), custom_call_target="tpu_custom_call" | custom-call | tf_op jit(solution)/shard_map/pallas_call | solution.py:1144
  83.5 0.8 copy.6
Async XLA Ops:
  0.0 0.7 copy-start.2
  0.7 1.0 %copy-start = (f32[8,8,8,1,2,128]{5,4,3,2,1,0:T(2,128)S(1)}, f32[8,8,8,1,2,128]{5,4,3,2,1,0:T(2,128)}, u32[]{:S(2)}) copy-start(f32[8,8,8,1,2,128]{5,4,3,2,1,0:T(2,128)} %param.3) | copy-start | bytes 1572868
  1.7 1.0 %copy-start.1 = (f32[872,128]{1,0:T(8,128)S(1)}, f32[872,128]{1,0:T(8,128)}, u32[]{:S(2)}) copy-start(f32[872,128]{1,0:T(8,128)} %constant.2.clone.cst_hbm) | copy-start | bytes 1339396
where the time goes:
time: 84.5 us; the launch traced here: 84.3 us
  Pallas kernels  80.8 us (96%)
  local copies, waits for them, and re-layouts  3.53 us (4%)
    pallas_call x1, Pallas kernels, local(): pl.pallas_call(kernel, out_shape=jax.ShapeDtypeStruct((rows, LANES), jnp....  80.8 us
    unnamed x7, local copies, waits for them, and re-layouts  3.53 us

commit v1 on v0

--- a/solution.py
+++ b/solution.py
@@ -228,8 +228,6 @@
     shapes["ein"] = pltpu.VMEM((PF * PF * PF * 2, LANES), f32)
     shapes["cst"] = pltpu.VMEM((CONSTS.row, LANES), f32)
     shapes["insem"] = pltpu.SemaphoreType.DMA((3,))
-    shapes["eout"] = pltpu.VMEM((PF * PF * PF * 2, LANES), f32)
-    shapes["outsem"] = pltpu.SemaphoreType.DMA((PF,))
     shapes["side"] = pltpu.VMEM((6, SUB, LANES), f32)
     shapes["dsrc"] = pltpu.VMEM((SUB, LANES), f32)
     shapes["dhalo"] = pltpu.VMEM((8, SUB, LANES), f32)
@@ -248,11 +246,11 @@
         shapes[tag + "c_s"] = pltpu.SemaphoreType.DMA((half,))
         shapes[tag + "c_r"] = pltpu.SemaphoreType.DMA((half,))
     nx, nz = n_dev + 1, 2 * n_node
-    for name in ("wx", "wxm", "wy", "wym", "wz", "wzm", "dg", "cx", "cr", "cq"):
-        shapes["c_" + name] = pltpu.VMEM((nx, nz, 2 * LANES), f32)
+    for name in ("wx", "wy", "wym", "wz", "wzm", "dg", "cx", "cr", "cq"):
+        shapes["c_" + name] = pltpu.VMEM((nx + 1, nz, LANES), f32)
+    shapes["c_wxm"] = pltpu.VMEM((nz, LANES), f32)
     shapes["c_main"] = pltpu.VMEM((nz, LANES), f32)
-    shapes["c_rest"] = pltpu.VMEM((nz, LANES), f32)
-    shapes["c_p"] = pltpu.VMEM((nx, nz + 2 * SUB, 2 * LANES), f32)
+    shapes["c_p"] = pltpu.VMEM((nx + 1, nz + 2 * SUB, LANES), f32)
     return shapes, low_rows
 
 
@@ -260,7 +258,7 @@
     half = n_node // 2
     nx, nz = n_dev + 1, 2 * n_node
 
-    def kernel(ein_hbm, diff_hbm, cst_hbm, out_hbm, *scratch):
+    def kernel(ein_hbm, diff_hbm, cst_hbm, out_ref, *scratch):
         s = dict(zip(names, scratch))
         node = lax.axis_index("node")
         dev = lax.axis_index("dev")
@@ -284,32 +282,21 @@
                 return s["cst"][row : row + size, :]
             return s["cst"][row + SUB * index : row + SUB * index + SUB, :]
 
-        def guarded(dx, fn):
-            if dx == 0:
-                fn()
-            else:
-                pl.when(has_lo if dx < 0 else has_hi)(fn)
-
         def neighbour(dx, dz):
-            return (lax.rem(node + dz + n_node, n_node), dev + dx)
+            return (lax.rem(node + dz + n_node, n_node), lax.rem(dev + dx + n_dev, n_dev))
 
         sibling = (node + 1 - 2 * lax.rem(node, 2), dev)
 
         def same_core(k):
             return lax.rem(node + 2 * k, n_node)
 
-        for tag in "fm":
-            for name in ("rx", "rz", "rc"):
-                s[name + tag][...] = jnp.zeros_like(s[name + tag])
-        s["dhalo"][...] = jnp.zeros_like(s["dhalo"])
-
         barrier = pltpu.get_barrier_semaphore()
 
         def greet(target):
             pl.semaphore_signal(barrier, inc=1, device_id=target, device_id_type=MESH)
 
         for dx, dz in DIRS:
-            guarded(dx, lambda dx=dx, dz=dz: greet(neighbour(dx, dz)))
+            greet(neighbour(dx, dz))
         far = lambda k: lax.rem(dev + k, n_dev)
 
         def greet_far(k, _):
@@ -322,10 +309,9 @@
 
         lax.fori_loop(1, n_dev, greet_far, 0)
         lax.fori_loop(1, half, greet_cores, 0)
-        ends = has_lo.astype(jnp.int32) + has_hi.astype(jnp.int32)
 
         def wait_barrier():
-            pl.semaphore_wait(barrier, n_dev - 1 + half - 1 + 2 + 3 * ends)
+            pl.semaphore_wait(barrier, n_dev - 1 + half - 1 + len(DIRS))
 
         def face_copy(tag, par, i):
             level = FINE if tag == "f" else MID
@@ -360,13 +346,13 @@
 
         def start_some(make, which):
             for i in which:
-                guarded(DIRS[i][0], lambda i=i: make(i).start())
+                make(i).start()
 
         def wait_some(make, which):
             for i in which:
-                guarded(DIRS[i][0], lambda i=i: make(i).wait_send())
+                make(i).wait_send()
             for i in which:
-                guarded(DIRS[OPP[i]][0], lambda i=i: make(i).wait_recv())
+                make(i).wait_recv()
 
         X_DIRS, Z_DIRS, EDGE_DIRS = (0, 1), (2, 3), (4, 5, 6, 7)
         parity = {"f": 0, "m": 0}
@@ -402,15 +388,18 @@
             wait_some(lambda i: face_copy(tag, par, i), which)
             buf, rx, rz, rc = (s[n + tag] for n in ("l", "rx", "rz", "rc"))
             last, top = level.points - 1, level.rows - SUB
+            has = (has_lo, has_hi)
             for side, a in ((0, 0), (1, last)):
                 for z, t in enumerate(unpack(tag, rx[par, side], level.planes)):
+                    t = jnp.where(has[side], t, 0.0)
                     buf[a, SUB * z : SUB * z + SUB, :] += t
             for side, row in ((0, 0), (1, top)):
                 for a, t in enumerate(unpack(tag, rz[par, side], level.points)):
                     buf[a, row : row + SUB, :] += t
             if edges:
                 for k, (a, row) in enumerate(((0, 0), (0, top), (last, 0), (last, top))):
-                    buf[a, row : row + SUB, :] += rc[par, k]
+                    t = jnp.where(has[0 if a == 0 else 1], rc[par, k], 0.0)
+                    buf[a, row : row + SUB, :] += t
 
         def sum_y(tag, a, first=0, count=None):
             level = FINE if tag == "f" else MID
@@ -474,6 +463,18 @@
                 device_id_type=MESH,
             )
 
+        def plane_rows(z):
+            if isinstance(z, int):
+                return slice(z * SUB, z * SUB + SUB)
+            return pl.ds(pl.multiple_of(z * SUB, SUB), SUB)
+
+        def each(tag, lower, upper, fn):
+            if tag == "m":
+                for k in range(lower, upper):
+                    fn(k)
+            else:
+                loop(lower, upper, fn)
+
         def loop(lower, upper, fn):
             def step(k, _):
                 fn(k)
@@ -532,7 +533,7 @@
             ends = (0, p - 1)
             even_row = 0.5 * (level.khat[0:1] + level.khat[0:1, ::-1])[:, : p // 2]
             odd_row = 0.5 * (level.khat[0:1] - level.khat[0:1, ::-1])[:, : p // 2]
-            x_edge, z_edge = {}, {}
+            x_edge, z_edge, x_out = {}, {}, []
             chunk = 5 if tag == "f" else n
             for z0 in range(0, n, chunk):
                 rows = slice(SUB * z0, SUB * (z0 + chunk))
@@ -554,8 +555,11 @@
                 put(dst, a, out)
                 out[0] = out[0] + s["side"][4] * x_edge[f, 0]
                 out[-1] = out[-1] + s["side"][5] * x_edge[f, 1]
-                put(s["sx" + tag], f, pack(tag, out))
-            start_faces(tag, X_DIRS)
+                x_out.append(out)
+                if tag == "f":
+                    put(s["sx" + tag], f, out)
+            if tag == "f":
+                start_faces(tag, X_DIRS)
             for side, row in ((0, 0), (1, top)):
                 rows = slice(row, row + SUB)
                 v = src[:, rows, :]
@@ -582,6 +586,10 @@
                     )
                 put(s["sz" + tag], side, pack(tag, out))
             start_faces(tag, Z_DIRS)
+            if tag == "m":
+                for f in range(2):
+                    put(s["sx" + tag], f, pack(tag, x_out[f]))
+                start_faces(tag, X_DIRS)
 
         def interior(tag, name, after=None):
             level = FINE if tag == "f" else MID
@@ -589,16 +597,19 @@
             src, dst = s[name + tag], s["l" + tag]
 
             def plane(z):
-                rows = pl.ds(pl.multiple_of(z * SUB, SUB), SUB)
+                rows = plane_rows(z)
                 v = src[:, rows, :]
                 acc = along_y(tag, v[1 : p - 1])
                 along_x = mix_even_odd(level.khat, [v[a] for a in range(p)])
                 weight = s["dz" + tag][rows, :]
-                mass = jnp.where(z == p - 1, 2.0 * SHIFT_MASS, SHIFT_MASS)
+                if isinstance(z, int):
+                    mass = 2.0 * SHIFT_MASS if z == p - 1 else SHIFT_MASS
+                else:
+                    mass = jnp.where(z == p - 1, 2.0 * SHIFT_MASS, SHIFT_MASS)
                 for a in range(1, p - 1):
                     dst[a, rows, :] = weight * (acc[a - 1] + along_x[a]) + mass * v[a]
 
-            loop(1, n - 1, plane)
+            each(tag, 1, n - 1, plane)
 
             def line(a):
                 out, _, _ = along_z(tag, src[a])
@@ -607,7 +618,7 @@
                 if after is not None:
                     after(a)
 
-            loop(1, p - 1, line)
+            each(tag, 1, p - 1, line)
 
         def apply(tag, name):
             level = FINE if tag == "f" else MID
@@ -615,7 +626,7 @@
             src, dst = s[name + tag], s["l" + tag]
 
             def plane(z):
-                rows = pl.ds(pl.multiple_of(z * SUB, SUB), SUB)
+                rows = plane_rows(z)
                 v = src[:, rows, :]
                 acc = along_y(tag, v)
                 along_x = mix_even_odd(level.khat, [v[a] for a in range(p)])
@@ -700,7 +711,7 @@
                 )
             start_faces(tag, Z_DIRS)
             before_inner()
-            loop(1, last, inner_update(tag, on))
+            each(tag, 1, last, inner_update(tag, on))
             before_faces()
             face_update(tag, on, True)
 
@@ -716,8 +727,6 @@
 
         ones = [has_lo.astype(jnp.float32), 1.0, has_hi.astype(jnp.float32)]
         copies = [1.0 + ones[0], 1.0, 1.0 + ones[2]]
-        levels = (("f", FINE), ("m", MID))
-
         def spread_row(row):
             return jnp.broadcast_to(row, (SUB, LANES))
 
@@ -725,7 +734,10 @@
             at = lambda dz: s["dhalo"].at[DIRS.index((dx, dz))]
             mid = s["dsrc"] if dx == 0 else at(0)
             rows = [at(-1)[1:2, :], mid[0:1, :], mid[1:2, :], at(1)[0:1, :]]
-            return [spread_row(row) for row in rows]
+            rows = [spread_row(row) for row in rows]
+            if dx != 0:
+                rows = [jnp.where(has_lo if dx < 0 else has_hi, row, 0.0) for row in rows]
+            return rows
 
         def kinds_of(q):
             return [q[0] + q[1], q[1], q[1] + q[2], q[2], q[2] + q[3]]
@@ -746,7 +758,7 @@
             diag = (float(level.kdiag[a]) + kzb) * s["cls" + tag][xc, rows, :]
             s["inv" + tag][a, rows, :] = 1.0 / (diag + copies[xc] * cnt)
 
-        def diagonals_inside():
+        def diagonals_inside(levels):
             first, second = spread_row(s["dsrc"][0:1, :]), spread_row(s["dsrc"][1:2, :])
             kinds = [first, first, first + second, second, second]
             for tag, level in levels:
@@ -759,12 +771,15 @@
                 for a in range(1, p - 1):
                     set_inverse(tag, level, a, 1, slice(SUB, level.rows - SUB))
 
-        def diagonals_faces():
+        def side_diffusivity():
             q = [patch(-1), patch(0), patch(1)]
             for side in range(2):
                 s["side"][side] = q[0][1 + side]
                 s["side"][2 + side] = q[2][1 + side]
                 s["side"][4 + side] = q[1][3 * side]
+
+        def diagonals_faces(levels):
+            q = [patch(-1), patch(0), patch(1)]
             xs = [[u + v for u, v in zip(q[0], q[1])], q[1], [u + v for u, v in zip(q[1], q[2])]]
             for xc in range(3):
                 kinds = kinds_of(xs[xc])
@@ -796,7 +811,7 @@
             loop(0, PF, line)
 
             def plane(z):
-                rows = pl.ds(pl.multiple_of(z * SUB, SUB), SUB)
+                rows = plane_rows(z)
                 v = s["tmpf"][:, rows, :]
                 t = jnp.stack(mix(R73, [v[a] for a in range(PF)]))
                 acc = const("r73", 0) * t
@@ -805,11 +820,11 @@
                 s["locm"][:, rows, :] = acc
                 s["lm"][:, rows, :] = acc
 
-            loop(0, MID.planes, plane)
+            each("m", 0, MID.planes, plane)
 
         def prolong_fine():
             def plane(z):
-                rows = pl.ds(pl.multiple_of(z * SUB, SUB), SUB)
+                rows = plane_rows(z)
                 v = s["xm"][:, rows, :]
                 acc = const("j73", 0) * v
                 for shift in range(1, SUB):
@@ -817,7 +832,7 @@
                 for a, t in enumerate(mix(J73, [acc[i] for i in range(PM)])):
                     s["tmpf"][a, rows, :] = t
 
-            loop(0, MID.planes, plane)
+            each("m", 0, MID.planes, plane)
 
             def line(a):
                 v = s["tmpf"][a]
@@ -862,38 +877,53 @@
                 mine[z * nx + 1 : z * nx + nx, :] += flat[:, 3 + z, :]
             mine[3 * nx : 3 * nx + 1, :] = jnp.sum(flat[:, 6, :], axis=0, keepdims=True)
 
-        def wide(rows):
-            return jnp.concatenate([rows, jnp.zeros_like(rows)], axis=1)
+        low_lane = lax.broadcasted_iota(jnp.int32, (nz, LANES), 1)
+        LAST = LANES - 1
+
+        def ahead(v):
+            return jnp.where(low_lane > 0, pltpu.roll(v, 1, 1), 0.0)
+
+        def to_end(x, v):
+            return jnp.where(low_lane == x, pltpu.roll(v, x + 1, 1), 0.0)
 
         def low_weights():
-            up_y = lambda v: pltpu.roll(v, 1, 1)
             up_z = lambda v: pltpu.roll(v, 1, 0)
             elem = lambda x: s["db"][pl.ds(x, nz, stride=n_dev), :]
-            zero = jnp.zeros((nz, 2 * LANES), jnp.float32)
-            lanes = lax.broadcasted_iota(jnp.int32, (nz, 2 * LANES), 1)
-            inside = (lanes <= LANES).astype(jnp.float32)
-            y_copies = (
-                inside + ((lanes > 0) & (lanes < LANES)).astype(jnp.float32)
-            )
+            zero = jnp.zeros((nz, LANES), jnp.float32)
+            y_copies = jnp.where(low_lane > 0, 2.0, 1.0)
+            end_wx = end_wy = end_wz = zero
             for x in range(nx):
-                lo = wide(elem(x - 1)) if x > 0 else zero
-                hi = wide(elem(x)) if x < n_dev else zero
+                lo = elem(x - 1) if x > 0 else zero
+                hi = elem(x) if x < n_dev else zero
                 both = lo + hi
                 wy = 0.5 * (both + up_z(both))
-                wz = 0.5 * (both + up_y(both))
+                wym = ahead(wy)
+                wz = 0.5 * (both + ahead(both))
+                wzm = up_z(wz)
+                hz = hi + up_z(hi)
+                wx = 0.5 * (hz + ahead(hz))
+                wxm = s["c_wx"][x - 1] if x > 0 else zero
                 s["c_wy"][x] = wy
-                s["c_wym"][x] = up_y(wy)
+                s["c_wym"][x] = wym
                 s["c_wz"][x] = wz
-                s["c_wzm"][x] = up_z(wz)
-                hz = hi + up_z(hi)
-                wx = 0.5 * (hz + up_y(hz))
+                s["c_wzm"][x] = wzm
                 s["c_wx"][x] = wx
-                wxm = s["c_wx"][x - 1] if x > 0 else zero
                 x_copies = 1.0 if x in (0, n_dev) else 2.0
-                s["c_dg"][x] = (
-                    wx + wxm + wy + s["c_wym"][x] + wz + s["c_wzm"][x]
-                    + 2.0 * SHIFT_MASS * x_copies * y_copies
-                )
+                s["c_dg"][x] = wx + wxm + wy + wym + wz + wzm + 2.0 * SHIFT_MASS * x_copies * y_copies
+                end_wx = end_wx + to_end(x, 0.5 * hz)
+                end_wy = end_wy + to_end(x, wy)
+                end_wz = end_wz + to_end(x, 0.5 * both)
+            end_wxm, end_wzm = ahead(end_wx), up_z(end_wz)
+            x_copies = jnp.where((low_lane == 0) | (low_lane == n_dev), 1.0, 2.0)
+            x_copies = jnp.where(low_lane < nx, x_copies, 0.0)
+            s["c_wx"][nx] = end_wx
+            s["c_wxm"][...] = end_wxm
+            s["c_wy"][nx] = end_wy
+            s["c_wz"][nx] = end_wz
+            s["c_wzm"][nx] = end_wzm
+            s["c_dg"][nx] = (
+                end_wx + end_wxm + end_wy + end_wz + end_wzm + 2.0 * SHIFT_MASS * x_copies
+            )
 
         def low_rhs():
             buf = s["gb"]
@@ -903,20 +933,19 @@
             at = lax.broadcasted_iota(jnp.int32, (n_node, LANES), 1)
             spare, spare_before = own(3 * nx), before(3 * nx)
 
-            def pick(rows, lane_index):
-                moved = rows if lane_index == 0 else pltpu.roll(rows, LANES - lane_index, 1)
-                return jnp.where(at == 0, moved, 0.0)
+            def pick(rows, first):
+                moved = rows if first == 0 else pltpu.roll(rows, LANES - first, 1)
+                return jnp.where(at < nx, moved, 0.0)
 
             even, odd = pl.ds(0, n_node, stride=2), pl.ds(1, n_node, stride=2)
-            left, right = pl.ds(0, LANES), pl.ds(LANES, LANES)
-            res, main, rest = s["c_cr"], s["c_main"], s["c_rest"]
+            res, main = s["c_cr"], s["c_main"]
             for x in range(nx):
                 main[even, :] = own(x) + before(2 * nx + x)
                 main[odd, :] = own(nx + x)
-                rest[even, :] = pick(spare, x) + pick(spare_before, 2 * nx + x)
-                rest[odd, :] = pick(spare, nx + x)
-                res[x, :, left] = main[...]
-                res[x, :, right] = rest[...]
+                res[x] = main[...]
+            main[even, :] = pick(spare, 0) + pick(spare_before, 2 * nx)
+            main[odd, :] = pick(spare, nx)
+            res[nx] = main[...]
 
         def fold(v):
             parts = [v[i : i + SUB] for i in range(0, v.shape[0], SUB)]
@@ -924,7 +953,7 @@
                 parts = [u + w for u, w in zip(parts[::2], parts[1::2])] + (
                     [parts[-1]] if len(parts) % 2 else []
                 )
-            return parts[0][:, :LANES] + parts[0][:, LANES:]
+            return parts[0]
 
         def total(v):
             return jnp.sum(v, axis=(0, 1), keepdims=True)
@@ -937,17 +966,22 @@
 
         def coarse_solve():
             p, q, res, sol = s["c_p"], s["c_cq"], s["c_cr"], s["c_cx"]
-            wide_lanes = 2 * LANES
             here = pl.ds(SUB, nz)
             norm = jnp.zeros((SUB, LANES), jnp.float32)
-            for x in range(nx):
+            for x in range(nx + 1):
                 v = res[x]
                 set_direction(x, v)
                 sol[x] = jnp.zeros_like(v)
                 norm = norm + fold(v * v)
 
+            def along_pipe(x):
+                out = s["c_wz"][x] * p[x, SUB + 1 : SUB + 1 + nz, :]
+                return out + s["c_wzm"][x] * p[x, SUB - 1 : SUB - 1 + nz, :]
+
             def iteration(_, now):
                 dot = jnp.zeros((SUB, LANES), jnp.float32)
+                end = p[nx, here, :]
+                last = jnp.zeros((nz, LANES), jnp.float32)
                 for x in range(nx):
                     v = p[x, here, :]
                     out = s["c_dg"][x] * v
@@ -955,22 +989,30 @@
                         out = out - s["c_wx"][x - 1] * p[x - 1, here, :]
                     if x < nx - 1:
                         out = out - s["c_wx"][x] * p[x + 1, here, :]
-                    out = out - s["c_wy"][x] * pltpu.roll(v, wide_lanes - 1, 1)
-                    out = out - s["c_wym"][x] * pltpu.roll(v, 1, 1)
-                    out = out - s["c_wz"][x] * p[x, SUB + 1 : SUB + 1 + nz, :]
-                    out = out - s["c_wzm"][x] * p[x, SUB - 1 : SUB - 1 + nz, :]
+                    above = jnp.where(
+                        low_lane == LAST, pltpu.roll(end, LAST - x, 1), pltpu.roll(v, LAST, 1)
+                    )
+                    below = pltpu.roll(v, 1, 1)
+                    out = out - s["c_wy"][x] * above - s["c_wym"][x] * below
+                    out = out - along_pipe(x)
                     q[x] = out
                     dot = dot + fold(v * out)
+                    last = jnp.where(low_lane == x, pltpu.roll(v, x + 1, 1), last)
+                out = s["c_dg"][nx] * end - s["c_wx"][nx] * pltpu.roll(end, LAST, 1)
+                out = out - s["c_wxm"][...] * pltpu.roll(end, 1, 1)
+                out = out - s["c_wy"][nx] * last - along_pipe(nx)
+                q[nx] = out
+                dot = dot + fold(end * out)
                 alpha = now / total(dot)
                 norm = jnp.zeros((SUB, LANES), jnp.float32)
-                for x in range(nx):
+                for x in range(nx + 1):
                     sol[x] += alpha * p[x, here, :]
                     v = res[x] - alpha * q[x]
                     res[x] = v
                     norm = norm + fold(v * v)
                 new = total(norm)
                 beta = new / now
-                for x in range(nx):
+                for x in range(nx + 1):
                     set_direction(x, res[x] + beta * p[x, here, :])
                 return new
 
@@ -986,10 +1028,9 @@
                         continue
                     x = jnp.clip(dev + i - 1, 0, n_dev)
                     z = lax.rem(2 * node + k - 1 + nz, nz)
-                    row = s["c_cx"][x, pl.ds(z, 1), :]
-                    row = jnp.broadcast_to(row, (SUB, 2 * LANES))
-                    low = row[:, :LANES]
-                    high = pltpu.roll(row, 2 * LANES - 1, 1)[:, :LANES]
+                    low = spread_row(s["c_cx"][x, pl.ds(z, 1), :])
+                    end = pltpu.roll(spread_row(s["c_cx"][nx, pl.ds(z, 1), :]), LAST - x, 1)
+                    high = jnp.where(lane < LAST, pltpu.roll(low, LAST, 1), end)
                     spread[i, k] = const("j31", 0) * low + const("j31", 1) * high
             left = mix(J31Z, [spread[0, k] for k in (1, 2, 3)])
             right = mix(J31Z, [spread[3, k] for k in (1, 2, 3)])
@@ -1032,8 +1073,6 @@
         nothing = lambda: None
         load_diff.wait()
         s["da"][dev] = s["dsrc"][...]
-        wait_barrier()
-        start_some(halo_copy, range(8))
         load_cst.wait()
         load_in.wait()
         wz = np.concatenate([FINE.w, FINE.w[1:]])
@@ -1058,20 +1097,25 @@
             return value
 
         loop(0, PF, load_line)
+        wait_barrier()
+        start_some(halo_copy, range(8))
 
         def halo_done():
             start_a("d")
             wait_some(halo_copy, range(8))
-            diagonals_faces()
+            diagonals_faces([("f", FINE)])
 
         def diff_stage_b():
+            diagonals_inside([("m", MID)])
+            diagonals_faces([("m", MID)])
             wait_a("d")
             mine = slot("d", node)
             for e in range(2):
                 mine[e * n_dev : (e + 1) * n_dev, :] = s["da"][:, e, :]
             start_b("d")
 
-        raw_round("f", update("f", "zero"), diagonals_inside, halo_done)
+        raw_round("f", update("f", "zero"), lambda: diagonals_inside([("f", FINE)]), halo_done)
+        side_diffusivity()
         steps("f", SMOOTH_FINE, "rhs", [diff_stage_b, lambda: forward_b("d")])
         apply("f", "x")
         restrict_fine()
@@ -1101,7 +1145,7 @@
             sum_y("m", a)
             first(a, slice(0, MID.rows))
 
-        loop(0, PM, first_mid)
+        each("m", 0, PM, first_mid)
         steps("m", SMOOTH_MID, "r", [nothing, nothing])
         prolong_fine()
         first = update("f", "first")
@@ -1112,24 +1156,16 @@
 
         chunk = PF * PF * 2
 
-        def out_copy(a):
-            rows = pl.ds(pl.multiple_of(a * chunk, chunk), chunk)
-            return pltpu.make_async_copy(
-                s["eout"].at[rows], out_hbm.at[rows], s["outsem"].at[a]
-            )
-
         def store_line(a):
             for e in range(2):
                 for c in range(PF):
                     z = e * (PF - 1) + c
                     start = a * chunk + 2 * c + e
-                    s["eout"][pl.ds(start, SUB, stride=2 * PF), :] = s["xf"][
+                    out_ref[pl.ds(start, SUB, stride=2 * PF), :] = s["xf"][
                         a, SUB * z : SUB * z + SUB, :
                     ]
-            out_copy(a).start()
 
         loop(0, PF, store_line)
-        loop(0, PF, lambda a: out_copy(a).wait())
 
     return kernel
 
@@ -1143,17 +1179,17 @@
     def local(element_load, diffusivity):
         out = pl.pallas_call(
             kernel,
-            out_shape=jax.ShapeDtypeStruct((rows, LANES), jnp.float32),
+            out_shape=pltpu.VMEM((rows, LANES), jnp.float32),
             in_specs=[pl.BlockSpec(memory_space=pltpu.HBM)] * 3,
-            out_specs=pl.BlockSpec(memory_space=pltpu.HBM),
+            out_specs=pl.BlockSpec(memory_space=pltpu.VMEM),
             scratch_shapes=list(shapes.values()),
             compiler_params=pltpu.CompilerParams(
                 collective_id=0, has_side_effects=True, vmem_limit_bytes=48 * 1024 * 1024
             ),
         )(
-            element_load.reshape(rows, LANES),
-            diffusivity.reshape(2, LANES),
-            jnp.asarray(CONSTS.array()),
+            pltpu.with_memory_space_constraint(element_load.reshape(rows, LANES), pltpu.HBM),
+            pltpu.with_memory_space_constraint(diffusivity.reshape(2, LANES), pltpu.HBM),
+            pltpu.with_memory_space_constraint(jnp.asarray(CONSTS.array()), pltpu.HBM),
         )
         return out.reshape(element_load.shape)
 

time: 84.5 us -> 79.2 us (0.937)
  local copies, waits for them, and re-layouts: 3.53 us -> 0.8 us
  Pallas kernels: 80.8 us -> 78.3 us
    unnamed x7 -> x1, local copies, waits for them, and re-layouts: 3.53 us -> 0.8 us
    pallas_call x1, Pallas kernels: 80.8 us -> 78.3 us  [local(): pl.pallas_call(kernel, out_shape=pltpu.VMEM((rows, LANES), jnp.float32),...]
where the time goes in v1:
time: 79.2 us; the launch traced here: 79.1 us
  Pallas kernels  78.3 us (99%)
  local copies, waits for them, and re-layouts  0.8 us (1%)
    pallas_call x1, Pallas kernels, local(): pl.pallas_call(kernel, out_shape=pltpu.VMEM((rows, LANES), jnp.float32),...  78.3 us

profile of v1, /device:TPU:32, one launch (start us, length us, event | category | flops | bytes accessed | tf_op | source)
XLA Modules:
  0.0 79.1 jit_solution(13885457933012986131)
XLA Ops:
  0.0 78.3 %shard_map.37 = f32[1024,128]{1,0:T(8,128)S(1)} custom-call(f32[1024,128]{1,0:T(8,128)} %bitcast.6, f32[2,128]{1,0:T(2,128)} %bitcast.7, f32[872,128]{1,0:T(8,128)} %constant.2.clone.cst_hbm), custom_call_target="tpu_custom_call" | custom-call | tf_op jit(solution)/shard_map/pallas_call | solution.py:1180
  78.3 0.8 %copy.6 = f32[8,8,8,1,2,128]{5,4,3,2,1,0:T(2,128)} copy(f32[8,8,8,1,2,128]{5,4,3,2,1,0:T(2,128)S(1)} %bitcast.5) | data formatting | bytes 1048576

commit v2 on v1

--- a/solution.py
+++ b/solution.py
@@ -227,7 +227,7 @@
     shapes["tmpm"] = pltpu.VMEM((PM, LOW.rows, LANES), f32)
     shapes["ein"] = pltpu.VMEM((PF * PF * PF * 2, LANES), f32)
     shapes["cst"] = pltpu.VMEM((CONSTS.row, LANES), f32)
-    shapes["insem"] = pltpu.SemaphoreType.DMA((3,))
+    shapes["insem"] = pltpu.SemaphoreType.DMA((PF + 2,))
     shapes["side"] = pltpu.VMEM((6, SUB, LANES), f32)
     shapes["dsrc"] = pltpu.VMEM((SUB, LANES), f32)
     shapes["dhalo"] = pltpu.VMEM((8, SUB, LANES), f32)
@@ -267,13 +267,19 @@
         has_lo, has_hi = dev > 0, dev < n_dev - 1
 
         s["dsrc"][...] = jnp.zeros_like(s["dsrc"])
+        chunk = PF * PF * 2
         load_diff = pltpu.make_async_copy(
-            diff_hbm, s["dsrc"].at[pl.ds(0, 2)], s["insem"].at[2]
+            diff_hbm, s["dsrc"].at[pl.ds(0, 2)], s["insem"].at[PF + 1]
         )
-        load_in = pltpu.make_async_copy(ein_hbm, s["ein"], s["insem"].at[0])
-        load_cst = pltpu.make_async_copy(cst_hbm, s["cst"], s["insem"].at[1])
+        load_cst = pltpu.make_async_copy(cst_hbm, s["cst"], s["insem"].at[PF])
+
+        def load_in(a):
+            rows = pl.ds(a * chunk, chunk)
+            return pltpu.make_async_copy(ein_hbm.at[rows], s["ein"].at[rows], s["insem"].at[a])
+
         load_diff.start()
-        load_in.start()
+        for a in (0, PF - 1) + tuple(range(1, PF - 1)):
+            load_in(a).start()
         load_cst.start()
 
         def const(name, index=None):
@@ -380,13 +386,12 @@
             for i, t in enumerate(parts):
                 ref[index, SUB * i : SUB * i + SUB, :] = t
 
-        def add_faces(tag, edges):
+        def add_faces(tag):
             level = FINE if tag == "f" else MID
             par = parity[tag]
             parity[tag] = 1 - par
-            which = X_DIRS + Z_DIRS + (EDGE_DIRS if edges else ())
-            wait_some(lambda i: face_copy(tag, par, i), which)
-            buf, rx, rz, rc = (s[n + tag] for n in ("l", "rx", "rz", "rc"))
+            wait_some(lambda i: face_copy(tag, par, i), X_DIRS + Z_DIRS)
+            buf, rx, rz = (s[n + tag] for n in ("l", "rx", "rz"))
             last, top = level.points - 1, level.rows - SUB
             has = (has_lo, has_hi)
             for side, a in ((0, 0), (1, last)):
@@ -396,10 +401,7 @@
             for side, row in ((0, 0), (1, top)):
                 for a, t in enumerate(unpack(tag, rz[par, side], level.points)):
                     buf[a, row : row + SUB, :] += t
-            if edges:
-                for k, (a, row) in enumerate(((0, 0), (0, top), (last, 0), (last, top))):
-                    t = jnp.where(has[0 if a == 0 else 1], rc[par, k], 0.0)
-                    buf[a, row : row + SUB, :] += t
+            return par
 
         def sum_y(tag, a, first=0, count=None):
             level = FINE if tag == "f" else MID
@@ -414,12 +416,15 @@
                 at < LANES - 1, pltpu.roll(lo, LANES - 1, 1), 0.0
             )
 
-        def sum_y_planes(tag, row):
+        def sum_y_planes(tag, row, which):
             p = (FINE if tag == "f" else MID).points
-            sel = (slice(1, p - 1), slice(row, row + SUB))
+            sel = (which, slice(row, row + SUB))
             t = s["l" + tag][sel]
-            up = pltpu.roll(pltpu.roll(t, 1, 2), SUB - p + 1, 1)
-            down = pltpu.roll(pltpu.roll(t, LANES - 1, 2), p - 1, 1)
+            across, along = t.ndim - 1, t.ndim - 2
+            up = pltpu.roll(t, 1, across)
+            down = pltpu.roll(t, LANES - 1, across)
+            up = pltpu.roll(up, SUB - p + 1, along)
+            down = pltpu.roll(down, p - 1, along)
             t = t + jnp.where((sub == 0) & (lane > 0), up, 0.0)
             t = t + jnp.where((sub == p - 1) & (lane < LANES - 1), down, 0.0)
             s["l" + tag][sel] = t
@@ -682,38 +687,52 @@
 
             return one
 
-        def face_update(tag, on, edges=False):
+        def face_update(tag, on):
             level = FINE if tag == "f" else MID
-            add_faces(tag, edges)
+            add_faces(tag)
             for a in (0, level.points - 1):
                 sum_y(tag, a)
                 on(a, slice(0, level.rows))
             for row in (0, level.rows - SUB):
-                sum_y_planes(tag, row)
+                sum_y_planes(tag, row, slice(1, level.points - 1))
                 on(slice(1, level.points - 1), slice(row, row + SUB))
 
-        def raw_round(tag, on, before_inner, before_faces):
+        def raw_start_x(tag):
+            level = FINE if tag == "f" else MID
+            buf = s["l" + tag]
+            start_faces(tag, EDGE_DIRS)
+            for f, a in ((0, 0), (1, level.points - 1)):
+                parts = [buf[a, SUB * z : SUB * z + SUB, :] for z in range(level.planes)]
+                put(s["sx" + tag], f, pack(tag, parts))
+            start_faces(tag, X_DIRS)
+
+        def raw_start_z(tag):
+            level = FINE if tag == "f" else MID
+            buf, top = s["l" + tag], level.rows - SUB
+            for side, row in ((0, 0), (1, top)):
+                parts = [buf[a, row : row + SUB, :] for a in range(level.points)]
+                put(s["sz" + tag], side, pack(tag, parts))
+            start_faces(tag, Z_DIRS)
+
+        def raw_finish(tag, on, before_faces, before_edges):
             level = FINE if tag == "f" else MID
             buf, last, top = s["l" + tag], level.points - 1, level.rows - SUB
-            start_faces(tag, EDGE_DIRS)
-            for f, a in ((0, 0), (1, last)):
-                put(
-                    s["sx" + tag],
-                    f,
-                    pack(tag, [buf[a, SUB * z : SUB * z + SUB, :] for z in range(level.planes)]),
-                )
-            start_faces(tag, X_DIRS)
-            for side, row in ((0, 0), (1, top)):
-                put(
-                    s["sz" + tag],
-                    side,
-                    pack(tag, [buf[a, row : row + SUB, :] for a in range(level.points)]),
-                )
-            start_faces(tag, Z_DIRS)
-            before_inner()
             each(tag, 1, last, inner_update(tag, on))
             before_faces()
-            face_update(tag, on, True)
+            par = add_faces(tag)
+            for a in (0, last):
+                sum_y(tag, a, 1, level.planes - 2)
+                on(a, slice(SUB, top))
+            for row in (0, top):
+                sum_y_planes(tag, row, slice(1, last))
+                on(slice(1, last), slice(row, row + SUB))
+            before_edges()
+            wait_some(lambda i: face_copy(tag, par, i), EDGE_DIRS)
+            for k, (a, row) in enumerate(((0, 0), (0, top), (last, 0), (last, top))):
+                rows = slice(row, row + SUB)
+                buf[a, rows, :] += jnp.where(has_lo if a == 0 else has_hi, s["rc" + tag][par, k], 0.0)
+                sum_y_planes(tag, row, a)
+                on(a, rows)
 
         def steps(tag, count, residual, between):
             coefs = (FINE if tag == "f" else MID).steps(count)
@@ -730,14 +749,16 @@
         def spread_row(row):
             return jnp.broadcast_to(row, (SUB, LANES))
 
+        def patch_row(dx, k):
+            dz, row = ((-1, 1), (0, 0), (0, 1), (1, 0))[k]
+            ref = s["dsrc"] if (dx, dz) == (0, 0) else s["dhalo"].at[DIRS.index((dx, dz))]
+            value = spread_row(ref[row : row + 1, :])
+            if dx != 0:
+                value = jnp.where(has_lo if dx < 0 else has_hi, value, 0.0)
+            return value
+
         def patch(dx):
-            at = lambda dz: s["dhalo"].at[DIRS.index((dx, dz))]
-            mid = s["dsrc"] if dx == 0 else at(0)
-            rows = [at(-1)[1:2, :], mid[0:1, :], mid[1:2, :], at(1)[0:1, :]]
-            rows = [spread_row(row) for row in rows]
-            if dx != 0:
-                rows = [jnp.where(has_lo if dx < 0 else has_hi, row, 0.0) for row in rows]
-            return rows
+            return [patch_row(dx, k) for k in range(4)]
 
         def kinds_of(q):
             return [q[0] + q[1], q[1], q[1] + q[2], q[2], q[2] + q[3]]
@@ -758,18 +779,44 @@
             diag = (float(level.kdiag[a]) + kzb) * s["cls" + tag][xc, rows, :]
             s["inv" + tag][a, rows, :] = 1.0 / (diag + copies[xc] * cnt)
 
-        def diagonals_inside(levels):
-            first, second = spread_row(s["dsrc"][0:1, :]), spread_row(s["dsrc"][1:2, :])
+        def set_class(tag, level, xc, kind, value):
+            full = nodal(value, level.points)
+            for z in range(level.planes):
+                if kind_of(z, level.points) == kind:
+                    s["cls" + tag][xc, SUB * z : SUB * z + SUB, :] = full
+
+        def diagonals_inside(tag, level):
+            first, second = patch_row(0, 1), patch_row(0, 2)
             kinds = [first, first, first + second, second, second]
-            for tag, level in levels:
-                p = level.points
-                full = [nodal(k, p) for k in kinds]
-                for z in range(level.planes):
-                    rows = slice(SUB * z, SUB * z + SUB)
-                    s["dz" + tag][rows, :] = kinds[kind_of(z, p)]
-                    s["cls" + tag][1, rows, :] = full[kind_of(z, p)]
-                for a in range(1, p - 1):
-                    set_inverse(tag, level, a, 1, slice(SUB, level.rows - SUB))
+            for z in range(level.planes):
+                s["dz" + tag][SUB * z : SUB * z + SUB, :] = kinds[kind_of(z, level.points)]
+            for kind in (1, 2, 3):
+                set_class(tag, level, 1, kind, kinds[kind])
+            for a in range(1, level.points - 1):
+                set_inverse(tag, level, a, 1, slice(SUB, level.rows - SUB))
+
+        def diagonals_x(tag, level):
+            for xc, dx, a in ((0, -1, 0), (2, 1, level.points - 1)):
+                first = patch_row(0, 1) + patch_row(dx, 1)
+                second = patch_row(0, 2) + patch_row(dx, 2)
+                for kind, value in ((1, first), (2, first + second), (3, second)):
+                    set_class(tag, level, xc, kind, value)
+                set_inverse(tag, level, a, xc, slice(SUB, level.rows - SUB))
+
+        def diagonals_z(tag, level):
+            set_class(tag, level, 1, 0, patch_row(0, 0) + patch_row(0, 1))
+            set_class(tag, level, 1, 4, patch_row(0, 2) + patch_row(0, 3))
+            for a in range(1, level.points - 1):
+                set_inverse(tag, level, a, 1, slice(0, SUB))
+                set_inverse(tag, level, a, 1, slice(level.rows - SUB, level.rows))
+
+        def diagonals_edges(tag, level):
+            for xc, dx, a in ((0, -1, 0), (2, 1, level.points - 1)):
+                q = [u + v for u, v in zip(patch(0), patch(dx))]
+                set_class(tag, level, xc, 0, q[0] + q[1])
+                set_class(tag, level, xc, 4, q[2] + q[3])
+                set_inverse(tag, level, a, xc, slice(0, SUB))
+                set_inverse(tag, level, a, xc, slice(level.rows - SUB, level.rows))
 
         def side_diffusivity():
             q = [patch(-1), patch(0), patch(1)]
@@ -777,29 +824,6 @@
                 s["side"][side] = q[0][1 + side]
                 s["side"][2 + side] = q[2][1 + side]
                 s["side"][4 + side] = q[1][3 * side]
-
-        def diagonals_faces(levels):
-            q = [patch(-1), patch(0), patch(1)]
-            xs = [[u + v for u, v in zip(q[0], q[1])], q[1], [u + v for u, v in zip(q[1], q[2])]]
-            for xc in range(3):
-                kinds = kinds_of(xs[xc])
-                for tag, level in levels:
-                    p = level.points
-                    full = [
-                        None if xc == 1 and i in (1, 2, 3) else nodal(k, p)
-                        for i, k in enumerate(kinds)
-                    ]
-                    for z in range(level.planes):
-                        value = full[kind_of(z, p)]
-                        if value is not None:
-                            s["cls" + tag][xc, SUB * z : SUB * z + SUB, :] = value
-            for tag, level in levels:
-                p, n = level.points, level.rows
-                set_inverse(tag, level, 0, 0, slice(0, n))
-                set_inverse(tag, level, p - 1, 2, slice(0, n))
-                for a in range(1, p - 1):
-                    set_inverse(tag, level, a, 1, slice(0, SUB))
-                    set_inverse(tag, level, a, 1, slice(n - SUB, n))
 
         def restrict_fine():
             def line(a):
@@ -978,7 +1002,7 @@
                 out = s["c_wz"][x] * p[x, SUB + 1 : SUB + 1 + nz, :]
                 return out + s["c_wzm"][x] * p[x, SUB - 1 : SUB - 1 + nz, :]
 
-            def iteration(_, now):
+            def step_length(now):
                 dot = jnp.zeros((SUB, LANES), jnp.float32)
                 end = p[nx, here, :]
                 last = jnp.zeros((nz, LANES), jnp.float32)
@@ -1003,7 +1027,10 @@
                 out = out - s["c_wy"][nx] * last - along_pipe(nx)
                 q[nx] = out
                 dot = dot + fold(end * out)
-                alpha = now / total(dot)
+                return now / total(dot)
+
+            def iteration(_, now):
+                alpha = step_length(now)
                 norm = jnp.zeros((SUB, LANES), jnp.float32)
                 for x in range(nx + 1):
                     sol[x] += alpha * p[x, here, :]
@@ -1016,7 +1043,9 @@
                     set_direction(x, res[x] + beta * p[x, here, :])
                 return new
 
-            lax.fori_loop(0, COARSE_ITERS, iteration, total(norm))
+            alpha = step_length(lax.fori_loop(0, COARSE_ITERS - 1, iteration, total(norm)))
+            for x in range(nx + 1):
+                sol[x] += alpha * p[x, here, :]
 
         def add_low():
             p, n = PM, MID.planes
@@ -1073,64 +1102,83 @@
         nothing = lambda: None
         load_diff.wait()
         s["da"][dev] = s["dsrc"][...]
-        load_cst.wait()
-        load_in.wait()
         wz = np.concatenate([FINE.w, FINE.w[1:]])
+
+        def mirrored(index, values):
+            out = jnp.float32(values[0])
+            for i in range(1, PF // 2):
+                out = jnp.where((index == i) | (index == PF - 1 - i), float(values[i]), out)
+            return out
+
+        across_y = mirrored(sub, 1.0 / FINE.w)
 
         def load_line(a):
             planes = []
             for e in range(2):
                 for c in range(PF):
-                    start = a * (PF * PF * 2) + 2 * c + e
+                    start = a * chunk + 2 * c + e
                     planes.append(s["ein"][pl.ds(start, SUB, stride=2 * PF), :])
             merged = planes[: PF - 1] + [planes[PF - 1] + planes[PF]] + planes[PF + 1 :]
-            scale = const("iwb") * wa_inverse(a)
+            scale = across_y * mirrored(jnp.int32(a), 1.0 / FINE.w)
             for z, v in enumerate(merged):
                 t = scale * v * float(1.0 / wz[z])
                 s["locf"][a, SUB * z : SUB * z + SUB, :] = t
                 s["lf"][a, SUB * z : SUB * z + SUB, :] = t
 
-        def wa_inverse(a):
-            value = jnp.float32(1.0 / FINE.w[0])
-            for i in range(1, PF // 2):
-                value = jnp.where((a == i) | (a == PF - 1 - i), 1.0 / FINE.w[i], value)
-            return value
-
-        loop(0, PF, load_line)
+        for a in (0, PF - 1):
+            load_in(a).wait()
+            load_line(a)
         wait_barrier()
         start_some(halo_copy, range(8))
-
-        def halo_done():
+        raw_start_x("f")
+        for a in range(1, PF - 1):
+            load_in(a).wait()
+        loop(1, PF - 1, load_line)
+        raw_start_z("f")
+        load_cst.wait()
+        diagonals_inside("f", FINE)
+        diagonals_inside("m", MID)
+
+        def halo_sides():
             start_a("d")
-            wait_some(halo_copy, range(8))
-            diagonals_faces([("f", FINE)])
+            wait_some(halo_copy, X_DIRS)
+            diagonals_x("f", FINE)
+            wait_some(halo_copy, Z_DIRS)
+            diagonals_z("f", FINE)
+
+        def halo_edges():
+            wait_some(halo_copy, EDGE_DIRS)
+            diagonals_edges("f", FINE)
 
         def diff_stage_b():
-            diagonals_inside([("m", MID)])
-            diagonals_faces([("m", MID)])
             wait_a("d")
             mine = slot("d", node)
             for e in range(2):
                 mine[e * n_dev : (e + 1) * n_dev, :] = s["da"][:, e, :]
             start_b("d")
 
-        raw_round("f", update("f", "zero"), lambda: diagonals_inside([("f", FINE)]), halo_done)
+        raw_finish("f", update("f", "zero"), halo_sides, halo_edges)
         side_diffusivity()
         steps("f", SMOOTH_FINE, "rhs", [diff_stage_b, lambda: forward_b("d")])
         apply("f", "x")
         restrict_fine()
 
-        def weights():
+        raw_start_x("m")
+        raw_start_z("m")
+
+        def order3_faces():
+            diagonals_x("m", MID)
+            diagonals_z("m", MID)
+            diagonals_edges("m", MID)
             wait_b("d")
-            low_weights()
-
-        raw_round("m", update("m", "zero"), nothing, weights)
-        steps("m", SMOOTH_MID, "rhs", [nothing, nothing])
+
+        raw_finish("m", update("m", "zero"), order3_faces, nothing)
+        steps("m", SMOOTH_MID, "rhs", [low_weights, nothing])
         faces("m", "x")
         interior("m", "x")
         restrict_mid()
         start_a("g")
-        add_faces("m", False)
+        add_faces("m")
         wait_a("g")
         sum_x_low()
         start_b("g")
@@ -1153,8 +1201,6 @@
         interior("f", "x", inner_update("f", first))
         face_update("f", first)
         steps("f", SMOOTH_FINE, "r", [nothing, nothing])
-
-        chunk = PF * PF * 2
 
         def store_line(a):
             for e in range(2):

time: 79.2 us -> 78.3 us (0.989)
  Pallas kernels: 78.3 us -> 77.4 us
    pallas_call x1, Pallas kernels: 78.3 us -> 77.4 us  [local(): pl.pallas_call(kernel, out_shape=pltpu.VMEM((rows, LANES), jnp.float32),...]
where the time goes in v2:
time: 78.3 us; the launch traced here: 78.2 us
  Pallas kernels  77.4 us (99%)
  local copies, waits for them, and re-layouts  0.8 us (1%)
    pallas_call x1, Pallas kernels, local(): pl.pallas_call(kernel, out_shape=pltpu.VMEM((rows, LANES), jnp.float32),...  77.4 us

profile of v2, /device:TPU:32, one launch (start us, length us, event | category | flops | bytes accessed | tf_op | source)
XLA Modules:
  0.0 78.2 jit_solution(7719664295677672576)
XLA Ops:
  0.0 77.4 %shard_map.37 = f32[1024,128]{1,0:T(8,128)S(1)} custom-call(f32[1024,128]{1,0:T(8,128)} %bitcast.6, f32[2,128]{1,0:T(2,128)} %bitcast.7, f32[872,128]{1,0:T(8,128)} %constant.2.clone.cst_hbm), custom_call_target="tpu_custom_call" | custom-call | tf_op jit(solution)/shard_map/pallas_call | solution.py:1226
  77.4 0.8 %copy.6 = f32[8,8,8,1,2,128]{5,4,3,2,1,0:T(2,128)} copy(f32[8,8,8,1,2,128]{5,4,3,2,1,0:T(2,128)S(1)} %bitcast.5) | data formatting | bytes 1048576

commit v3 on v2

--- a/solution.py
+++ b/solution.py
@@ -172,6 +172,9 @@
     mz[[0, level.points - 1, -1]] = 2
     CONSTS.add("cnt" + tag, (SHIFT_MASS * mz[:, None, None] * my[None]).reshape(-1, LANES))
     CONSTS.add("mz" + tag, np.repeat(SHIFT_MASS * plane_sum(level.points), SUB))
+MID_COPIES = np.ones(MID.planes)
+MID_COPIES[[0, PM - 1, -1]] = 2
+CONSTS.add("mzfull", np.repeat(SHIFT_MASS * MID_COPIES, SUB))
 CONSTS.add("r73", np.concatenate(roll_coefs(R73)))
 CONSTS.add("j73", np.concatenate(roll_coefs(J73)))
 CONSTS.add("r31", np.concatenate(roll_coefs(R31)))
@@ -228,6 +231,8 @@
     shapes["ein"] = pltpu.VMEM((PF * PF * PF * 2, LANES), f32)
     shapes["cst"] = pltpu.VMEM((CONSTS.row, LANES), f32)
     shapes["insem"] = pltpu.SemaphoreType.DMA((PF + 2,))
+    shapes["ghost_x"] = pltpu.VMEM((2, 3, MID.planes, SUB, LANES), f32)
+    shapes["ghost_z"] = pltpu.VMEM((2, 3, PM, SUB, LANES), f32)
     shapes["side"] = pltpu.VMEM((6, SUB, LANES), f32)
     shapes["dsrc"] = pltpu.VMEM((SUB, LANES), f32)
     shapes["dhalo"] = pltpu.VMEM((8, SUB, LANES), f32)
@@ -734,9 +739,11 @@
                 sum_y_planes(tag, row, a)
                 on(a, rows)
 
-        def steps(tag, count, residual, between):
+        def steps(tag, count, residual, between, done=0):
             coefs = (FINE if tag == "f" else MID).steps(count)
             for index, (c1, c2) in enumerate(coefs):
+                if index < done:
+                    continue
                 on = update(tag, "next", c1, c2, index == count - 2, residual)
                 residual = "r"
                 faces(tag, "d")
@@ -1047,57 +1054,247 @@
             for x in range(nx + 1):
                 sol[x] += alpha * p[x, here, :]
 
-        def add_low():
-            p, n = PM, MID.planes
-            h = float((MID.khat @ J31)[0, 0])
-            spread = {}
-            for i in range(4):
-                for k in range(5):
-                    if i in (0, 3) and k in (0, 4):
-                        continue
-                    x = jnp.clip(dev + i - 1, 0, n_dev)
-                    z = lax.rem(2 * node + k - 1 + nz, nz)
-                    low = spread_row(s["c_cx"][x, pl.ds(z, 1), :])
-                    end = pltpu.roll(spread_row(s["c_cx"][nx, pl.ds(z, 1), :]), LAST - x, 1)
-                    high = jnp.where(lane < LAST, pltpu.roll(low, LAST, 1), end)
-                    spread[i, k] = const("j31", 0) * low + const("j31", 1) * high
-            left = mix(J31Z, [spread[0, k] for k in (1, 2, 3)])
-            right = mix(J31Z, [spread[3, k] for k in (1, 2, 3)])
-            inner = [
-                mix(J31, [spread[1, k], spread[2, k]]) for k in range(5)
-            ]
-            q = [patch(-1), patch(0), patch(1)]
-            xs = [[u + v for u, v in zip(q[0], q[1])], q[1], [u + v for u, v in zip(q[1], q[2])]]
-            along_x = [kinds_of(v) for v in q]
-            lines = [mix(J31Z, [inner[k][a] for k in (1, 2, 3)]) for a in range(p)]
-            for a in range(p):
-                xc = 0 if a == 0 else 2 if a == p - 1 else 1
-                w, u = xs[xc], lines[a]
-                kinds = kinds_of(w)
-                ends = (0, p - 1, n - 1)
-                slope = [u[0] - inner[0][a], u[p - 1] - u[0], u[n - 1] - u[p - 1], inner[4][a] - u[n - 1]]
-                flow = [v * t for v, t in zip(w, slope)]
-                for z in range(n):
-                    rows = slice(SUB * z, SUB * z + SUB)
-                    kind = kind_of(z, p)
-                    copies_z = 2.0 if z in ends else 1.0
-                    out = kinds[kind] * along_y("m", u[z][None])[0]
-                    out = out + (SHIFT_MASS * copies_z * copies[xc]) * u[z]
-                    if z in ends:
-                        k = ends.index(z)
-                        out = out + h * (flow[k] - flow[k + 1])
-                    if a == 0:
-                        out = out + h * (
-                            along_x[0][kind] * (u[z] - left[z])
-                            + along_x[1][kind] * (u[z] - lines[p - 1][z])
-                        )
-                    if a == p - 1:
-                        out = out + h * (
-                            along_x[1][kind] * (u[z] - lines[0][z])
-                            + along_x[2][kind] * (u[z] - right[z])
-                        )
-                    s["lm"][a, rows, :] += out
-                    s["xm"][a, rows, :] += u[z]
+        n3, edge_slope = MID.planes, float((MID.khat @ J31)[0, 0])
+
+        def stacked(parts):
+            return jnp.stack(list(parts))
+
+        def exists(o):
+            return (dev + o >= 0) & (dev + o < n_dev)
+
+        def diff_at(o, k):
+            x = jnp.clip(dev + o, 0, n_dev - 1)
+            z = lax.rem(2 * node + k + nz, nz)
+            row = spread_row(s["db"][pl.ds(z * n_dev + x, 1), :])
+            return row if o == 0 else jnp.where(exists(o), row, 0.0)
+
+        def over_planes(q):
+            kinds = kinds_of(q)
+            return stacked(kinds[kind_of(z, PM)] for z in range(n3))
+
+        def column(o):
+            return [diff_at(o, k) for k in (-1, 0, 1, 2)]
+
+        def add_rows(p, q):
+            return [u + v for u, v in zip(p, q)]
+
+        def copies_at(o, a):
+            if a == 0:
+                return 1.0 + exists(o - 1).astype(jnp.float32)
+            if a == PM - 1:
+                return 1.0 + exists(o + 1).astype(jnp.float32)
+            return 1.0
+
+        def around(o, a):
+            q = column(o)
+            if a == 0:
+                q = add_rows(q, column(o - 1))
+            if a == PM - 1:
+                q = add_rows(q, column(o + 1))
+            return q
+
+        def spread_low(i, k):
+            x = jnp.clip(dev + i, 0, n_dev)
+            z = lax.rem(2 * node + k + nz, nz)
+            low = spread_row(s["c_cx"][x, pl.ds(z, 1), :])
+            end = pltpu.roll(spread_row(s["c_cx"][nx, pl.ds(z, 1), :]), LAST - x, 1)
+            high = jnp.where(lane < LAST, pltpu.roll(low, LAST, 1), end)
+            return const("j31", 0) * low + const("j31", 1) * high
+
+        def once(fn):
+            seen = {}
+
+            def get(*key):
+                if key not in seen:
+                    seen[key] = fn(*key)
+                return seen[key]
+
+            return get
+
+        def y_summed(v):
+            across, along = v.ndim - 1, v.ndim - 2
+            up = pltpu.roll(pltpu.roll(v, 1, across), SUB - PM + 1, along)
+            down = pltpu.roll(pltpu.roll(v, LANES - 1, across), PM - 1, along)
+            v = v + jnp.where((sub == 0) & (lane > 0), up, 0.0)
+            return v + jnp.where((sub == PM - 1) & (lane < LANES - 1), down, 0.0)
+
+        def low_tools():
+            node_at = once(spread_low)
+            line_at = once(lambda i: stacked(mix(J31Z, [node_at(i, k) for k in (0, 1, 2)])))
+            mass = const("mzfull").reshape(n3, SUB, LANES)
+            h = edge_slope
+
+            def along_line(o, a):
+                pick = lambda f: mix(J31[a : a + 1], [f(o), f(o + 1)])[0]
+                u = pick(line_at)
+                before, after = pick(lambda i: node_at(i, -1)), pick(lambda i: node_at(i, 3))
+                w = around(o, a)
+                out = over_planes(w) * along_y("m", u) + copies_at(o, a) * mass * u
+                f0, f1 = w[0] * (u[0] - before), w[1] * (u[PM - 1] - u[0])
+                f2, f3 = w[2] * (u[n3 - 1] - u[PM - 1]), w[3] * (after - u[n3 - 1])
+                zero = jnp.zeros((SUB, LANES), jnp.float32)
+                flow = [zero] * n3
+                flow[0], flow[PM - 1], flow[n3 - 1] = f0 - f1, f1 - f2, f2 - f3
+                out = out + h * stacked(flow)
+                if a in (0, PM - 1):
+                    inner = line_at(o + 1) if a == 0 else line_at(o)
+                    outer_o = o - 1 if a == 0 else o + 1
+                    outer = line_at(o - 1) if a == 0 else line_at(o + 2)
+                    out = out + h * (
+                        over_planes(column(o)) * (u - inner)
+                        + over_planes(column(outer_o)) * (u - outer)
+                    )
+                return u, out
+
+            def beyond_z(side, c):
+                k = -1 if side == 0 else 2
+                far = c == (0 if side == 0 else PM - 1)
+                other = k - 1 if side == 0 else k + 1
+                at_x = once(lambda i: mix(J31[c : c + 1], [node_at(i, k), node_at(i, k + 1)])[0])
+                across = lambda kk: stacked(mix(J31, [node_at(0, kk), node_at(1, kk)]))
+                weights = once(lambda o: diff_at(o, k) + diff_at(o, other) if far else diff_at(o, k))
+                u = stacked(mix(J31, [at_x(0), at_x(1)]))
+                sums = lambda f: stacked(
+                    [f(0) + f(-1), f(0), f(0), f(0) + f(1)]
+                )
+                total_w = sums(weights)
+                copies3 = [copies_at(0, a) * (2.0 if far else 1.0) * SHIFT_MASS for a in range(PM)]
+                out = total_w * along_y("m", u) + stacked(copies3[a] * u[a] for a in range(PM))
+                zero = jnp.zeros((SUB, LANES), jnp.float32)
+                flow = [zero] * PM
+                flow[0] = weights(-1) * (u[0] - at_x(-1)) + weights(0) * (u[0] - u[PM - 1])
+                flow[PM - 1] = weights(0) * (u[PM - 1] - u[0]) + weights(1) * (u[PM - 1] - at_x(2))
+                out = out + h * stacked(flow)
+                if far:
+                    inner, outer = (across(k + 1), across(k - 1)) if side == 0 else (
+                        across(k),
+                        across(k + 2),
+                    )
+                    out = out + h * (
+                        sums(lambda o: diff_at(o, k)) * (u - inner)
+                        + sums(lambda o: diff_at(o, other)) * (u - outer)
+                    )
+                return out
+
+            return along_line, beyond_z
+
+        beyond_x = ((-1, (0, 1, 2), MID.khat[PM - 1]), (1, (1, 2, 3), MID.khat[0]))
+        beyond_c = (((0, 1, 2), MID.khat[PM - 1]), ((1, 2, 3), MID.khat[0]))
+
+        def ghost_diagonals():
+            theta = MID.theta
+            my = 1.0 + jnp.where(((sub == 0) & (lane > 0)) | ((sub == PM - 1) & (lane < LAST)), 1.0, 0.0)
+            kb = mirrored_rows(MID.kdiag)
+            kz = [float(v) for v in np.concatenate([MID.kdiag, MID.kdiag[1:]])]
+            for side, (o, points, row) in enumerate(beyond_x):
+                for index, a in enumerate(points):
+                    kinds = [nodal(k, PM) for k in kinds_of(around(o, a))]
+                    for z in range(n3):
+                        diag = (float(MID.kdiag[a]) + kz[z] + kb) * kinds[kind_of(z, PM)]
+                        diag = diag + (float(MID_COPIES[z]) * SHIFT_MASS * copies_at(o, a)) * my
+                        s["ghost_x"][side, index, z] = float(row[a] / theta) / diag
+            for side, (planes, row) in enumerate(beyond_c):
+                k = -1 if side == 0 else 2
+                other = k - 1 if side == 0 else k + 1
+                for index, c in enumerate(planes):
+                    far = c in (0, PM - 1)
+                    weights = lambda o: diff_at(o, k) + diff_at(o, other) if far else diff_at(o, k)
+                    for a in range(PM):
+                        w = weights(0)
+                        if a in (0, PM - 1):
+                            w = w + weights(-1 if a == 0 else 1)
+                        diag = (float(MID.kdiag[a] + MID.kdiag[c]) + kb) * nodal(w, PM)
+                        scale = (2.0 if far else 1.0) * SHIFT_MASS * copies_at(0, a)
+                        s["ghost_z"][side, index, a] = float(row[c] / theta) / (diag + scale * my)
+
+        def mirrored_rows(values):
+            out = jnp.zeros((SUB, LANES), jnp.float32)
+            for i, v in enumerate(values):
+                out = jnp.where(sub == i, float(v), out)
+            return out
+
+        def send_known_part():
+            c = float(1.0 / MID.theta)
+            for a in range(PM):
+                sum_y("m", a)
+                res = s["rhsm"][a] - s["lm"][a]
+                s["rm"][a] = res
+                s["dm"][a] = c * s["invm"][a] * res
+            plane = lambda z: s["dm"][:, SUB * z : SUB * z + SUB, :]
+            for side, (points, row) in enumerate(((range(1, PM), 0), (range(PM - 1), PM - 1))):
+                rows = [s["dm"][a] for a in points]
+                t = mix(MID.khat[row : row + 1, list(points)], rows)[0]
+                put(s["sxm"], side, pack("m", [t[SUB * z : SUB * z + SUB] for z in range(n3)]))
+                first = 0 if side == 0 else PM - 1
+                t = mix(MID.khat[row : row + 1, list(points)], [plane(first + c) for c in points])[0]
+                put(s["szm"], side, pack("m", [t[a] for a in range(PM)]))
+            start_faces("m", X_DIRS + Z_DIRS)
+
+        def after_coarse(c1, c2):
+            c = float(1.0 / MID.theta)
+            along_line, beyond_z = low_tools()
+            shape = (n3, SUB, LANES)
+            flat = (MID.rows, LANES)
+            par = parity["m"]
+            parity["m"] = 1 - par
+            for a in range(PM):
+                u, rho = along_line(0, a)
+                res = s["rm"][a] - y_summed(rho).reshape(flat)
+                upd = c * s["invm"][a] * res
+                s["rm"][a] = res
+                s["dm"][a] = upd
+                s["xm"][a] = s["xm"][a] + u.reshape(flat) + upd
+            for side, (o, points, row) in enumerate(beyond_x):
+                acc = None
+                for index, a in enumerate(points):
+                    _, rho = along_line(o, a)
+                    t = s["ghost_x"][side, index] * y_summed(rho)
+                    acc = t if acc is None else acc + t
+                s["tmpf"][side] = acc.reshape(flat)
+            for side, (planes, row) in enumerate(beyond_c):
+                acc = None
+                for index, cc in enumerate(planes):
+                    t = s["ghost_z"][side, index] * y_summed(beyond_z(side, cc))
+                    acc = t if acc is None else acc + t
+                s["tmpf"][2 + side, 0 : PM * SUB, :] = acc.reshape(PM * SUB, LANES)
+            wait_some(lambda i: face_copy("m", par, i), X_DIRS + Z_DIRS)
+            d = [s["dm"][a].reshape(shape) for a in range(PM)]
+            own_x = mix_even_odd(MID.khat, d)
+            last = float(MID.khat[PM - 1, PM - 1])
+            terms_x = []
+            for side, a in ((0, 0), (1, PM - 1)):
+                t = stacked(unpack("m", s["rxm"][par, side], n3)) - s["tmpf"][side].reshape(shape)
+                terms_x.append(t + last * d[a])
+            terms_z = []
+            for side, z in ((0, 0), (1, n3 - 1)):
+                t = stacked(unpack("m", s["rzm"][par, side], PM))
+                t = t - s["tmpf"][2 + side, 0 : PM * SUB, :].reshape(PM, SUB, LANES)
+                terms_z.append(t + last * stacked(v[z] for v in d))
+            mass = const("mzfull").reshape(shape)
+            here = over_planes(column(0))
+            for a in range(PM):
+                w = around(0, a)
+                out = over_planes(w) * along_y("m", d[a]) + copies_at(0, a) * mass * d[a]
+                out = out + here * own_x[a]
+                if a == 0:
+                    out = out + over_planes(column(-1)) * terms_x[0]
+                if a == PM - 1:
+                    out = out + over_planes(column(1)) * terms_x[1]
+                low = mix_even_odd(MID.khat, [d[a][z] for z in range(PM)])
+                high = mix_even_odd(MID.khat, [d[a][z] for z in range(PM - 1, n3)])
+                along = [w[1] * v for v in low] + [w[2] * v for v in high[1:]]
+                along[PM - 1] = along[PM - 1] + w[2] * high[0]
+                along[0] = along[0] + w[0] * terms_z[0][a]
+                along[n3 - 1] = along[n3 - 1] + w[3] * terms_z[1][a]
+                out = y_summed(out + stacked(along)).reshape(flat)
+                res = s["rm"][a] - out
+                upd = c1 * s["dm"][a] + c2 * s["invm"][a] * res
+                s["lm"][a] = res
+                s["locm"][a] = upd
+            for a in range(PM):
+                s["rm"][a] = s["lm"][a]
+                s["dm"][a] = s["locm"][a]
+                s["xm"][a] = s["xm"][a] + s["locm"][a]
 
         nothing = lambda: None
         load_diff.wait()
@@ -1173,12 +1370,13 @@
             wait_b("d")
 
         raw_finish("m", update("m", "zero"), order3_faces, nothing)
-        steps("m", SMOOTH_MID, "rhs", [low_weights, nothing])
+        steps("m", SMOOTH_MID, "rhs", [low_weights, ghost_diagonals])
         faces("m", "x")
         interior("m", "x")
         restrict_mid()
         start_a("g")
         add_faces("m")
+        send_known_part()
         wait_a("g")
         sum_x_low()
         start_b("g")
@@ -1186,15 +1384,9 @@
         wait_b("g")
         low_rhs()
         coarse_solve()
-        add_low()
-        first = update("m", "first")
-
-        def first_mid(a):
-            sum_y("m", a)
-            first(a, slice(0, MID.rows))
-
-        each("m", 0, PM, first_mid)
-        steps("m", SMOOTH_MID, "r", [nothing, nothing])
+        coefs = MID.steps(SMOOTH_MID)
+        after_coarse(*coefs[0])
+        steps("m", SMOOTH_MID, "r", [nothing, nothing], 1)
         prolong_fine()
         first = update("f", "first")
         faces("f", "x")

time: 78.3 us -> 74.5 us (0.951)
  Pallas kernels: 77.4 us -> 73.6 us
    pallas_call x1, Pallas kernels: 77.4 us -> 73.6 us  [local(): pl.pallas_call(kernel, out_shape=pltpu.VMEM((rows, LANES), jnp.float32),...]
where the time goes in v3:
time: 74.5 us; the launch traced here: 74.4 us
  Pallas kernels  73.6 us (99%)
  local copies, waits for them, and re-layouts  0.8 us (1%)
    pallas_call x1, Pallas kernels, local(): pl.pallas_call(kernel, out_shape=pltpu.VMEM((rows, LANES), jnp.float32),...  73.6 us

profile of v3, /device:TPU:32, one launch (start us, length us, event | category | flops | bytes accessed | tf_op | source)
XLA Modules:
  0.0 74.4 jit_solution(2296502148474795089)
XLA Ops:
  0.0 73.6 %shard_map.37 = f32[1024,128]{1,0:T(8,128)S(1)} custom-call(f32[1024,128]{1,0:T(8,128)} %bitcast.6, f32[2,128]{1,0:T(2,128)} %bitcast.7, f32[928,128]{1,0:T(8,128)} %constant.2.clone.cst_hbm), custom_call_target="tpu_custom_call" | custom-call | tf_op jit(solution)/shard_map/pallas_call | solution.py:1418
  73.6 0.8 %copy.6 = f32[8,8,8,1,2,128]{5,4,3,2,1,0:T(2,128)} copy(f32[8,8,8,1,2,128]{5,4,3,2,1,0:T(2,128)S(1)} %bitcast.5) | data formatting | bytes 1048576

commit v4 on v3

--- a/solution.py
+++ b/solution.py
@@ -271,6 +271,27 @@
         lane = lax.broadcasted_iota(jnp.int32, (SUB, LANES), 1)
         has_lo, has_hi = dev > 0, dev < n_dev - 1
 
+        def const(name, index=None):
+            row, size = CONSTS.at[name]
+            if index is None:
+                return s["cst"][row : row + size, :]
+            return s["cst"][row + SUB * index : row + SUB * index + SUB, :]
+
+        def neighbour(dx, dz):
+            return (lax.rem(node + dz + n_node, n_node), lax.rem(dev + dx + n_dev, n_dev))
+
+        sibling = (node + 1 - 2 * lax.rem(node, 2), dev)
+
+        def same_core(k):
+            return lax.rem(node + 2 * k, n_node)
+
+        barrier = pltpu.get_barrier_semaphore()
+
+        def greet(target):
+            pl.semaphore_signal(barrier, inc=1, device_id=target, device_id_type=MESH)
+
+        for dx, dz in DIRS:
+            greet(neighbour(dx, dz))
         s["dsrc"][...] = jnp.zeros_like(s["dsrc"])
         chunk = PF * PF * 2
         load_diff = pltpu.make_async_copy(
@@ -287,27 +308,6 @@
             load_in(a).start()
         load_cst.start()
 
-        def const(name, index=None):
-            row, size = CONSTS.at[name]
-            if index is None:
-                return s["cst"][row : row + size, :]
-            return s["cst"][row + SUB * index : row + SUB * index + SUB, :]
-
-        def neighbour(dx, dz):
-            return (lax.rem(node + dz + n_node, n_node), lax.rem(dev + dx + n_dev, n_dev))
-
-        sibling = (node + 1 - 2 * lax.rem(node, 2), dev)
-
-        def same_core(k):
-            return lax.rem(node + 2 * k, n_node)
-
-        barrier = pltpu.get_barrier_semaphore()
-
-        def greet(target):
-            pl.semaphore_signal(barrier, inc=1, device_id=target, device_id_type=MESH)
-
-        for dx, dz in DIRS:
-            greet(neighbour(dx, dz))
         far = lambda k: lax.rem(dev + k, n_dev)
 
         def greet_far(k, _):
@@ -532,7 +532,7 @@
             out = [first * t for t in low[: p - 1]]
             out.append(first * low[p - 1] + second * high[0])
             out += [second * t for t in high[1:]]
-            return out, low[0], high[-1]
+            return out
 
         def faces(tag, name):
             level = FINE if tag == "f" else MID
@@ -543,33 +543,7 @@
             ends = (0, p - 1)
             even_row = 0.5 * (level.khat[0:1] + level.khat[0:1, ::-1])[:, : p // 2]
             odd_row = 0.5 * (level.khat[0:1] - level.khat[0:1, ::-1])[:, : p // 2]
-            x_edge, z_edge, x_out = {}, {}, []
-            chunk = 5 if tag == "f" else n
-            for z0 in range(0, n, chunk):
-                rows = slice(SUB * z0, SUB * (z0 + chunk))
-                v = [src[a, rows, :] for a in range(p)]
-                even = mix(even_row, [v[i] + v[p - 1 - i] for i in range(p // 2)])[0]
-                odd = mix(odd_row, [v[i] - v[p - 1 - i] for i in range(p // 2)])[0]
-                for f, xt in ((0, even + odd), (1, even - odd)):
-                    if z0 == 0:
-                        x_edge[f, 0] = xt[0:SUB]
-                    if z0 + chunk == n:
-                        x_edge[f, 1] = xt[-SUB:]
-                    u = v[ends[f]]
-                    yt = along_y(tag, u.reshape(chunk, SUB, LANES)).reshape(chunk * SUB, LANES)
-                    mass = s["cst"][mass_row + SUB * z0 : mass_row + SUB * (z0 + chunk), :]
-                    dst[ends[f], rows, :] = dz[rows, :] * (xt + yt) + mass * u
-            for f, a in enumerate(ends):
-                out, z_edge[f, 0], z_edge[f, 1] = along_z(tag, src[a])
-                out = [t + dst[a, SUB * z : SUB * z + SUB, :] for z, t in enumerate(out)]
-                put(dst, a, out)
-                out[0] = out[0] + s["side"][4] * x_edge[f, 0]
-                out[-1] = out[-1] + s["side"][5] * x_edge[f, 1]
-                x_out.append(out)
-                if tag == "f":
-                    put(s["sx" + tag], f, out)
-            if tag == "f":
-                start_faces(tag, X_DIRS)
+            x_edge = {}
             for side, row in ((0, 0), (1, top)):
                 rows = slice(row, row + SUB)
                 v = src[:, rows, :]
@@ -579,27 +553,42 @@
                 zt = mix(
                     level.khat[p - 1 : p] if side else level.khat[0:1],
                     [
-                        src[1 : p - 1, SUB * (plane0 + c) : SUB * (plane0 + c) + SUB, :]
+                        src[:, SUB * (plane0 + c) : SUB * (plane0 + c) + SUB, :]
                         for c in range(p)
                     ],
                 )[0]
                 weight = dz[rows, :]
-                out = [None] * p
+                out = [weight * (xt[a] + yt[a] + zt[a]) + SHIFT_MASS * v[a] for a in range(p)]
                 for a in range(1, p - 1):
-                    out[a] = weight * (xt[a] + yt[a] + zt[a - 1]) + SHIFT_MASS * v[a]
                     dst[a, rows, :] = out[a]
                 for f, a in enumerate(ends):
+                    x_edge[f, side] = xt[a]
                     out[a] = (
-                        dst[a, rows, :]
-                        + s["side"][2 * f + side] * (z_edge[f, side] + yt[a])
+                        out[a]
+                        + s["side"][2 * f + side] * (zt[a] + yt[a])
                         + (SHIFT_MASS * has[f]) * v[a]
                     )
                 put(s["sz" + tag], side, pack(tag, out))
             start_faces(tag, Z_DIRS)
-            if tag == "m":
-                for f in range(2):
-                    put(s["sx" + tag], f, pack(tag, x_out[f]))
-                start_faces(tag, X_DIRS)
+            chunk = 5 if tag == "f" else n
+            for z0 in range(0, n, chunk):
+                rows = slice(SUB * z0, SUB * (z0 + chunk))
+                v = [src[a, rows, :] for a in range(p)]
+                even = mix(even_row, [v[i] + v[p - 1 - i] for i in range(p // 2)])[0]
+                odd = mix(odd_row, [v[i] - v[p - 1 - i] for i in range(p // 2)])[0]
+                for f, xt in ((0, even + odd), (1, even - odd)):
+                    u = v[ends[f]]
+                    yt = along_y(tag, u.reshape(chunk, SUB, LANES)).reshape(chunk * SUB, LANES)
+                    mass = s["cst"][mass_row + SUB * z0 : mass_row + SUB * (z0 + chunk), :]
+                    dst[ends[f], rows, :] = dz[rows, :] * (xt + yt) + mass * u
+            for f, a in enumerate(ends):
+                out = along_z(tag, src[a])
+                out = [t + dst[a, SUB * z : SUB * z + SUB, :] for z, t in enumerate(out)]
+                put(dst, a, out)
+                out[0] = out[0] + s["side"][4] * x_edge[f, 0]
+                out[-1] = out[-1] + s["side"][5] * x_edge[f, 1]
+                put(s["sx" + tag], f, pack(tag, out))
+            start_faces(tag, X_DIRS)
 
         def interior(tag, name, after=None):
             level = FINE if tag == "f" else MID
@@ -622,7 +611,7 @@
             each(tag, 1, n - 1, plane)
 
             def line(a):
-                out, _, _ = along_z(tag, src[a])
+                out = along_z(tag, src[a])
                 for i in range(1, n - 1):
                     dst[a, SUB * i : SUB * i + SUB, :] += out[i]
                 if after is not None:
@@ -648,7 +637,7 @@
             loop(0, n, plane)
 
             def line(a):
-                out, _, _ = along_z(tag, src[a])
+                out = along_z(tag, src[a])
                 for i in range(n):
                     dst[a, SUB * i : SUB * i + SUB, :] += out[i]
 

time: 74.5 us -> 73.3 us (0.984)
  Pallas kernels: 73.6 us -> 72.4 us
    pallas_call x1, Pallas kernels: 73.6 us -> 72.4 us  [local(): pl.pallas_call(kernel, out_shape=pltpu.VMEM((rows, LANES), jnp.float32),...]
where the time goes in v4:
time: 73.3 us; the launch traced here: 73.2 us
  Pallas kernels  72.4 us (99%)
  local copies, waits for them, and re-layouts  0.8 us (1%)
    pallas_call x1, Pallas kernels, local(): pl.pallas_call(kernel, out_shape=pltpu.VMEM((rows, LANES), jnp.float32),...  72.4 us

profile of v4, /device:TPU:32, one launch (start us, length us, event | category | flops | bytes accessed | tf_op | source)
XLA Modules:
  0.0 73.2 jit_solution(369631303777715092)
XLA Ops:
  0.0 72.4 %shard_map.37 = f32[1024,128]{1,0:T(8,128)S(1)} custom-call(f32[1024,128]{1,0:T(8,128)} %bitcast.6, f32[2,128]{1,0:T(2,128)} %bitcast.7, f32[928,128]{1,0:T(8,128)} %constant.2.clone.cst_hbm), custom_call_target="tpu_custom_call" | custom-call | tf_op jit(solution)/shard_map/pallas_call | solution.py:1407
  72.4 0.8 %copy.6 = f32[8,8,8,1,2,128]{5,4,3,2,1,0:T(2,128)} copy(f32[8,8,8,1,2,128]{5,4,3,2,1,0:T(2,128)S(1)} %bitcast.5) | data formatting | bytes 1048576

commit v5 on v4

--- a/solution.py
+++ b/solution.py
@@ -492,14 +492,25 @@
 
             lax.fori_loop(lower, upper, step, 0)
 
+        def ring(k, size):
+            return min(k % size, -k % size)
+
+        side = 4 if half % 4 == 0 else half
+        far_first_dev = sorted(range(1, n_dev), key=lambda k: -ring(k, n_dev))
+        far_first_node = sorted(
+            range(1, half), key=lambda k: -(ring(k % side, side) + ring(k // side, half // side))
+        )
+
         def start_a(tag):
-            loop(1, n_dev, lambda k: gather_a(tag, k).start())
+            for k in far_first_dev:
+                gather_a(tag, k).start()
 
         def wait_a(tag):
             loop(1, n_dev, lambda k: gather_a(tag, k).wait())
 
         def start_b(tag):
-            loop(1, half, lambda k: gather_b(tag, k).start())
+            for k in far_first_node:
+                gather_b(tag, k).start()
             gather_c(tag, 0).start()
 
         def forward_b(tag):
@@ -507,7 +518,8 @@
                 gather_b(tag, k).wait_recv()
                 gather_c(tag, k).start()
 
-            loop(1, half, one)
+            for k in far_first_node[::-1]:
+                one(k)
 
         def wait_b(tag):
             loop(1, half, lambda k: gather_b(tag, k).wait_send())
@@ -694,7 +706,6 @@
         def raw_start_x(tag):
             level = FINE if tag == "f" else MID
             buf = s["l" + tag]
-            start_faces(tag, EDGE_DIRS)
             for f, a in ((0, 0), (1, level.points - 1)):
                 parts = [buf[a, SUB * z : SUB * z + SUB, :] for z in range(level.planes)]
                 put(s["sx" + tag], f, pack(tag, parts))
@@ -1316,6 +1327,7 @@
             load_line(a)
         wait_barrier()
         start_some(halo_copy, range(8))
+        start_faces("f", EDGE_DIRS)
         raw_start_x("f")
         for a in range(1, PF - 1):
             load_in(a).wait()
@@ -1349,8 +1361,9 @@
         apply("f", "x")
         restrict_fine()
 
+        start_faces("m", EDGE_DIRS)
+        raw_start_z("m")
         raw_start_x("m")
-        raw_start_z("m")
 
         def order3_faces():
             diagonals_x("m", MID)

time: 73.3 us -> 73.8 us (level)
  no operation moved by 1% of the time
where the time goes in v5:
time: 73.8 us; the launch traced here: 73.7 us
  Pallas kernels  72.9 us (99%)
  local copies, waits for them, and re-layouts  0.8 us (1%)
    pallas_call x1, Pallas kernels, local(): pl.pallas_call(kernel, out_shape=pltpu.VMEM((rows, LANES), jnp.float32),...  72.9 us

profile of v5, /device:TPU:32, one launch (start us, length us, event | category | flops | bytes accessed | tf_op | source)
XLA Modules:
  0.0 73.7 jit_solution(1288571308434838524)
XLA Ops:
  0.0 72.9 %shard_map.37 = f32[1024,128]{1,0:T(8,128)S(1)} custom-call(f32[1024,128]{1,0:T(8,128)} %bitcast.6, f32[2,128]{1,0:T(2,128)} %bitcast.7, f32[928,128]{1,0:T(8,128)} %constant.2.clone.cst_hbm), custom_call_target="tpu_custom_call" | custom-call | tf_op jit(solution)/shard_map/pallas_call | solution.py:1420
  72.9 0.8 %copy.6 = f32[8,8,8,1,2,128]{5,4,3,2,1,0:T(2,128)} copy(f32[8,8,8,1,2,128]{5,4,3,2,1,0:T(2,128)S(1)} %bitcast.5) | data formatting | bytes 1048576
